TPU v7x, 32 devices: a whole 2x2x4 slice. The times are simulated.
32 devices in a mesh: group: 2 (over y), lat: 8 (over z, x), lon: 2 (over core).
Axes of the slice: x: 2, y: 2, z: 4, core: 2. Of those that a mesh axis runs over, the one named last changes fastest.
Arguments:
- tracers: float32 [8, 32, 32, 1152], P('group', None, 'lat', 'lon'), parts along dimension 0, may hold values from -6 to 6
- courant_lat: float32 [64, 32, 1152], P('group', 'lat', 'lon'), parts along dimension 0, may hold values from -0.45 to 0.45
- courant_lon: float32 [64, 32, 1152], P('group', 'lat', 'lon'), parts along dimension 0, may hold values from -0.45 to 0.45
- surface_flux: float32 [8, 32, 1152], P('group', 'lat', 'lon'), parts along dimension 0, may hold values from -6 to 6
- mixing: float32 [32, 32], replicated, may hold values from -1 to 1
- decay_rate: float32 [4, 32], replicated, may hold values from 0.05 to 1
- owners: int32 [16, 2, 18, 1], P(('group', 'lat'), 'lon'), parts along dimension 0, may hold values from 0 to 7; in each aligned block of 18 rows (0 to 17, 18 to 35, ..., all dimensions but the last counted through in order) at most 5 rows name the same one
- polar_mask: int32 [64], P(('group', 'lat')), parts along dimension 0, may hold values 0 or 1
Outputs:
- tracers_out: float32 [8, 32, 32, 1152], P('group', None, 'lat', 'lon'), parts along dimension 0
- owner_energy: float32 [16, 2], P(('group', 'lat'), 'lon'), parts along dimension 0
There are 2 independent parts, one for each index of `group`. A program takes and returns all parts, laid end to end along the dimension named above; an argument that names none is the same for every part. Nothing has to cross between parts.
Inputs may be any that keep to these rules, and one draw needn't show every extreme that they name: `owners`: the 18 blocks of one lat index and one lon index name one owner at most 5 times; in every draw some lat and lon index names one owner exactly 5 times.
All inputs are finite; a program needn't handle non-finite values. No bound on the sum of `polar_mask` on one device may be relied on, other than what follows from the above.
Results may differ from a plain program's by a relative error of at most 0.000073.
Values sent between devices are 32-bit elements; how exact they have to be, the bound alone decides.
No kernel may reach another device: no remote copies, remote signals or barrier semaphores. Data moves between devices by JAX's collectives and lax.ppermute only.
A program may use at most 128 MiB of HBM per device.

v0:
```python
import math

import jax
import jax.numpy as jnp
from jax import lax
from jax.sharding import PartitionSpec as P

NLON = 1152
BLOCK = 128


def padded_2(block, sides, width, periodic):
    for axis, dim in sides:
        count = lax.axis_size(axis)
        forward = [(i, i + 1) for i in range(count - 1)]
        if periodic:
            forward.append((count - 1, 0))
        backward = [(target, source) for source, target in forward]
        low = lax.ppermute(
            lax.slice_in_dim(block, block.shape[dim] - width, None, axis=dim), axis, forward
        )
        high = lax.ppermute(lax.slice_in_dim(block, 0, width, axis=dim), axis, backward)
        block = jnp.concatenate([low, block, high], axis=dim)
    return block


def edges_along(padded, cell_count, along_dim):

    def window(offset):
        return lax.slice_in_dim(padded, offset, offset + cell_count + 1, axis=along_dim)

    return 7.0 / 12.0 * (window(2) + window(1)) - 1.0 / 12.0 * (window(3) + window(0))


def transport(tracers, lat_padded, lat_courant, lon_padded, lon_courant, first_row):
    band_rows = tracers.shape[2]
    sector = tracers.shape[3]
    lat_edges = edges_along(lat_padded, band_rows, 2)
    pole_mask = (first_row + jnp.arange(band_rows + 1) > 0).astype(jnp.float32)
    lat_flux = lat_courant[None] * lat_edges * pole_mask[:, None]
    lon_edges = edges_along(lon_padded, sector, 3)
    lon_flux = lon_courant[None] * lon_edges
    return (
        tracers
        - (lat_flux[:, :, 1:] - lat_flux[:, :, :-1])
        - (lon_flux[..., 1:] - lon_flux[..., :-1])
    )


def column_physics(columns, surface_part, mixing, decay_rate):
    mixed_state = jnp.einsum("kl,...tlc->...tkc", mixing, columns, precision=lax.Precision.HIGHEST)
    mixed_state = mixed_state.at[..., -1, :].add(surface_part)
    result = mixed_state / (1.0 + decay_rate[:, :, None] * mixed_state * mixed_state)
    energy = jnp.sum((result - columns) ** 2, axis=(-3, -2, -1))
    return (result, energy)


def fourier_table(length):
    position = jnp.arange(length)[:, None]
    column = jnp.arange(length)[None, :]
    half_wave = length // 2
    is_cosine = column <= half_wave
    wavenumber = jnp.where(is_cosine, column, column - half_wave)
    phase_index = position * wavenumber % length
    radians = 2.0 * math.pi / length * phase_index.astype(jnp.float32)
    return jnp.where(is_cosine, jnp.cos(radians), jnp.sin(radians))


def spectral_scale(length, row_ids, total_rows):
    column = jnp.arange(length)
    half_wave = length // 2
    is_cosine = column <= half_wave
    wavenumber = jnp.where(is_cosine, column, column - half_wave)
    is_end = is_cosine & ((wavenumber == 0) | (wavenumber == half_wave))
    weight = jnp.where(is_end, 1.0 / length, 2.0 / length)
    latitude = (-0.5 + (row_ids.astype(jnp.float32) + 0.5) / total_rows) * math.pi
    sine = jnp.sin(math.pi * wavenumber.astype(jnp.float32) / length)
    ratio_sq = (2.0 * jnp.cos(latitude)[:, None] / jnp.where(wavenumber == 0, 1.0, sine)[None]) ** 2
    damping = jnp.where(wavenumber[None] == 0, 1.0, jnp.minimum(1.0, ratio_sq))
    return weight[None] * damping


def on_device(
    tracers, courant_lat, courant_lon, surface_flux, mixing, decay_rate, owners, polar_mask
):
    tracer_count, level_count, band_rows, sector = tracers.shape
    first_row = lax.axis_index("lat") * band_rows
    stacked_lat = jnp.concatenate([tracers, courant_lat[None]], axis=0)
    lat_full = padded_2(stacked_lat, (("lat", 2),), 2, False)
    stacked_lon = jnp.concatenate([tracers, courant_lon[None]], axis=0)
    lon_full = padded_2(stacked_lon, (("lon", 3),), 2, True)
    lat_courant = lat_full[tracer_count, :, 2 : band_rows + 3]
    lon_courant = lon_full[tracer_count, :, :, 2 : sector + 3]
    advected = transport(
        tracers,
        lat_full[:tracer_count],
        lat_courant,
        lon_full[:tracer_count],
        lon_courant,
        first_row,
    )
    block_count = band_rows * sector // BLOCK
    blocks = advected.reshape(tracer_count, level_count, block_count, BLOCK).transpose(2, 0, 1, 3)
    surface_blocks = surface_flux.reshape(tracer_count, block_count, BLOCK).transpose(1, 0, 2)
    owner_ids = owners.reshape(block_count)
    lat_count = lax.axis_size("lat")
    onehot = (owner_ids[:, None] == jnp.arange(lat_count)[None]).astype(jnp.float32)
    physics_blocks, block_energy = column_physics(blocks, surface_blocks, mixing, decay_rate)
    partial_energy = jnp.dot(block_energy, onehot, precision=lax.Precision.HIGHEST)
    owner_total = lax.psum_scatter(partial_energy, "lat", scatter_dimension=0, tiled=True)
    owner_energy = (owner_total / (block_count * BLOCK)).reshape(1, 1)
    physics_grid = physics_blocks.transpose(1, 2, 0, 3).reshape(
        tracer_count, level_count, band_rows, sector
    )
    basis_table = fourier_table(NLON)
    total_rows = lat_count * band_rows
    row_scale = spectral_scale(NLON, first_row + jnp.arange(band_rows), total_rows)
    spectra = jnp.einsum(
        "tkrx,xm->tkrm",
        lax.all_gather(physics_grid, "lon", axis=3, tiled=True),
        basis_table,
        precision=lax.Precision.HIGHEST,
    )
    own_table = lax.dynamic_slice_in_dim(basis_table, lax.axis_index("lon") * sector, sector, 0)
    filtered = jnp.einsum(
        "tkrm,xm->tkrx", spectra * row_scale, own_table, precision=lax.Precision.HIGHEST
    )
    tracers_out = jnp.where(polar_mask[:, None] == 1, filtered, physics_grid)
    return (tracers_out, owner_energy)


def solution(mesh):
    placed = (
        P("group", None, "lat", "lon"),
        P("group", "lat", "lon"),
        P("group", "lat", "lon"),
        P("group", "lat", "lon"),
        P(),
        P(),
        P(("group", "lat"), "lon", None, None),
        P(("group", "lat")),
    )
    return jax.shard_map(
        on_device,
        mesh=mesh,
        in_specs=placed,
        out_specs=(P("group", None, "lat", "lon"), P(("group", "lat"), "lon")),
        check_vma=False,
    )
```

profile of v0, /device:TPU:0, one launch (start us, length us, event | category | flops | bytes accessed | tf_op | source)
XLA Modules:
  0.0 150.9 jit_solution(1981301866236908208)
XLA Ops:
  7.2 0.0 copy-start
  7.2 0.0 copy-start.3
  7.2 0.0 all-gather.2.cloned.1.call-start
  7.2 1.5 copy.20
  8.7 0.0 copy-done.3
  8.8 0.0 copy-start.4
  8.8 1.3 fusion.37
  10.1 1.3 collective-permute-start
  11.4 6.4 %collective-permute-start.1 = (f32[5,32,2,576]{3,1,2,0:T(8,128)}, f32[5,32,2,576]{3,1,2,0:T(8,128)}, u32[]{:S(2)}, u32[]{:S(2)}) collective-permute-start(f32[5,32,2,576]{3,1,2,0:T(8,128)} %get-tuple-element.23), channel_id=1, source_target_pairs={{0,2},{2,4},{4,6},{6,8},{8,10},{10,12},{12,14},{1,3},{3,5},{5,7},{... | collective-permute-start | bytes 2211848 | tf_op jit(solution)/shard_map/ppermute | solution.py:19
  17.8 0.0 copy-done.4
  17.8 0.8 fusion.38
  18.7 0.0 collective-permute-start.2
  18.7 0.5 collective-permute-start.3
  19.2 0.5 fusion.44
  19.7 0.0 copy-start.6
  19.7 0.0 copy-start.5
  19.8 22.6 %fusion.55 = f32[1152,1152,1,1]{1,0,3,2:T(8,128)} fusion(s32[1152]{0:T(1024)S(1)} %add_select_fusion.1, pred[1152]{0:T(1024)(128)(4,1)S(1)} %iota_compare_fusion.2), kind=kLoop, calls=%fused_computation.5.clone.clone.clone.1 | loop fusion | flops 13271040 | bytes 5314176 | tf_op jit(solution)/shard_map/tkrx,xm->tkrm/dot_general | solution.py:118
  42.4 0.0 copy-done.6
  42.4 0.5 compare_convert_fusion
  42.9 0.0 copy-done.5
  42.9 0.1 reshape.170
  43.0 0.0 collective-permute-done.2
  43.0 0.1 maximum_bitcast_fusion.1
  43.1 0.0 collective-permute-done.3
  43.1 1.6 %pad_maximum_fusion.1 = (f32[5,32,4,578]{3,1,2,0:T(8,128)S(1)}, f32[5,32,4,578]{3,1,2,0:T(8,128)S(1)}) fusion(f32[5,32,4,2]{3,1,2,0:T(8,128)S(1)} %collective-permute-done.2, f32[1,32,4,576]{3,1,2,0:T(8,128)S(1)} %bitcast.64, f32[4,32,4,576]{3,1,2,0:T(8,128)S(1)} %copy.20, f32[5,32,4,2]{3,1,2,0:T(8,128)} %collective-permute-done.3), kind=kLoop, calls=%fused_computation.29 | loop fusion | flops 1479680 | bytes 4444160 | tf_op jit(solution)/shard_map/concatenate | solution.py:23
  44.8 0.7 fusion.27
  45.5 0.0 collective-permute-done
  45.6 0.0 copy-start.10
  45.6 5.6 %collective-permute-done.1 = f32[5,32,2,576]{3,1,2,0:T(8,128)} collective-permute-done((f32[5,32,2,576]{3,1,2,0:T(8,128)}, f32[5,32,2,576]{3,1,2,0:T(8,128)}, u32[]{:S(2)}, u32[]{:S(2)}) %collective-permute-start.1) | collective-permute-done | bytes 737312 | tf_op jit(solution)/shard_map/ppermute | solution.py:19
  51.2 1.8 %pad_maximum_fusion = (f32[5,32,6,576]{3,1,2,0:T(8,128)S(1)}, f32[5,32,6,576]{3,1,2,0:T(8,128)S(1)}) fusion(f32[5,32,2,576]{3,1,2,0:T(8,128)S(1)} %collective-permute-done, f32[1,32,4,576]{3,1,2,0:T(8,128)S(1)} %bitcast.61, f32[4,32,4,576]{3,1,2,0:T(8,128)S(1)} %copy.20, f32[5,32,2,576]{3,1,2,0:T(8,128)} %collective-permute-done.1), kind=kLoop, calls=%fused_computation.15 | loop fusion | flops 2211840 | bytes 7372800 | tf_op jit(solution)/shard_map/concatenate | solution.py:23
  53.0 0.0 copy-done.10
  53.0 0.0 copy-start.2
  53.0 0.5 fusion.19
  53.4 0.8 copy-done.2
  54.3 0.6 fusion.24
  54.9 0.8 copy.23
  55.7 1.1 reshape.168
  56.9 0.0 copy-done
  56.9 0.0 copy-start.9
  56.9 1.2 fusion.32
  58.2 2.1 %scatter-add.4 = f32[18,4,32,128]{3,2,1,0:T(8,128)S(1)} dynamic-update-slice(f32[18,4,32,128]{3,2,1,0:T(8,128)S(1)} %bitcast.65, f32[18,4,1,128]{3,2,1,0:T(1,128)S(1)} %bitcast.66, s32[]{:T(128)} %constant.83.clone.1, s32[]{:T(128)} %constant.83.clone.1, s32[]{:T(128)} %constant.84.clone.1, s32[]{:T(128)} %constant.83.clone.1) | dynamic-update-slice | bytes 73732 | tf_op jit(solution)/shard_map/scatter-add | solution.py:52
  60.3 0.0 copy-done.9
  60.3 0.6 fusion.35
  60.9 0.7 copy.27
  61.6 0.8 reshape.171
  62.4 3.5 %copy.28 = f32[4,32,4,576]{1,2,0,3:T(4,128)} copy(f32[4,32,4,576]{3,2,1,0:T(4,128)S(1)} %reshape.171) | data formatting | bytes 2359296 | tf_op jit(solution)/shard_map/reshape | solution.py:112
  65.9 0.0 all-gather.2.cloned.1.call-update
  65.9 0.1 cosine_multiply_fusion
  66.0 0.1 sine_select_fusion.2
  66.1 0.5 copy-done.11
  66.6 0.0 copy-done.8
  66.6 0.1 fusion.42
  66.7 0.0 copy-start.12
  66.7 0.0 copy-start.13
  66.7 22.6 %sine_select_fusion = f32[1152,1152]{1,0:T(8,128)} fusion(s32[1152]{0:T(1024)S(1)} %add_select_fusion.1, pred[1152]{0:T(1024)(128)(4,1)S(1)} %copy-done.7), kind=kLoop, calls=%fused_computation.6 | loop fusion | flops 13271040 | bytes 5314176 | tf_op jit(solution)/shard_map/jit(_where)/select_n | solution.py:66
  89.3 0.2 convolution_bitcast_fusion
  89.5 0.0 copy-done.13
  89.5 0.6 dynamic-slice.10
  90.1 19.9 %all-reduce = f32[8]{0:T(128)S(1)} all-reduce(f32[8]{0:T(128)S(1)} %convolution_bitcast_fusion), channel_id=2, replica_groups=mesh['group'=2,'lat'=8,'lon'=2] {'lat'}, use_global_device_ids=true, to_apply=%region_1.0.clone | all-reduce | flops 8 | bytes 64
  110.0 1.2 dynamic-slice.11
  111.8 0.0 all-gather.2.cloned.1.call-done
  111.9 22.8 %fusion.8 = f32[4,32,4,1152]{3,1,2,0:T(8,128)S(1)} fusion(f32[4,32,4,1152]{1,2,0,3:T(4,128)} %all-gather.2.cloned.1.call-done, f32[4,1152]{1,0:T(4,128)S(1)} %fusion.42, f32[1152,1152,1,1]{1,0,3,2:T(8,128)} %fusion.55), kind=kOutput, calls=%fused_computation.11 | convolution fusion | flops 8154316800 | bytes 10045440 | tf_op jit(solution)/shard_map/tkrx,xm->tkrm/dot_general | solution.py:118
  134.7 6.4 %fusion.21 = f32[4,32,4,576]{3,1,2,0:T(8,128)S(1)} fusion(f32[4,32,4,1152]{3,1,2,0:T(8,128)S(1)} %fusion.8, f32[1152,1152]{1,0:T(8,128)S(1)} %copy-done.1, s32[]{:T(128)S(6)} %select_n.80, f32[4,32,4,576]{3,2,1,0:T(4,128)S(1)} %reshape.171, pred[4]{0:T(512)(128)(4,1)S(1)} %broadcast_compare_fusion), kind=kOutput, calls=%fused_computation.31 | convolution fusion | flops 4077158400 | bytes 7504388 | tf_op jit(solution)/shard_map/tkrm,xm->tkrx/dot_general | solution.py:125
  141.0 1.9 %copy.31 = f32[4,32,4,576]{3,2,1,0:T(4,128)} copy(f32[4,32,4,576]{3,1,2,0:T(8,128)S(1)} %fusion.21) | data formatting | bytes 2359296
  (15 shorter events, 0.2 us)
Async XLA Ops:
  7.2 49.7 %copy-start = (f32[32,32]{1,0:T(8,128)S(1)}, f32[32,32]{1,0:T(8,128)}, u32[]{:S(2)}) copy-start(f32[32,32]{1,0:T(8,128)} %param.14) | copy-start | bytes 12292
  7.2 1.6 %copy-start.3 = (f32[32,4,576]{2,1,0:T(4,128)S(1)}, f32[32,4,576]{2,1,0:T(4,128)}, u32[]{:S(2)}) copy-start(f32[32,4,576]{2,1,0:T(4,128)} %param.11) | copy-start | bytes 884740
  7.2 104.7 %all-gather.2.cloned.1.call-start = ((), (), s32[]{:S(2)}) async-start(), calls=%async_computation | async-start | bytes 14155776 | tf_op jit(solution)/shard_map/all_gather | solution.py:120
  8.8 9.0 %copy-start.4 = (f32[32,4,576]{2,1,0:T(4,128)S(1)}, f32[32,4,576]{2,1,0:T(4,128)}, u32[]{:S(2)}) copy-start(f32[32,4,576]{2,1,0:T(4,128)} %param.12) | copy-start | bytes 884740
  10.1 35.4 %collective-permute-start = (f32[5,32,2,576]{3,1,2,0:T(8,128)}, f32[5,32,2,576]{3,1,2,0:T(8,128)S(1)}, u32[]{:S(2)}, u32[]{:S(2)}) collective-permute-start(f32[5,32,2,576]{3,1,2,0:T(8,128)} %get-tuple-element.22), channel_id=1, source_target_pairs={{2,0},{4,2},{6,4},{8,6},{10,8},{12,10},{14,12},{3,1},{5,3},{7,5},{... | collective-permute-start | bytes 2211848 | tf_op jit(solution)/shard_map/ppermute | solution.py:22
  11.4 39.8 %collective-permute-start.1 = (f32[5,32,2,576]{3,1,2,0:T(8,128)}, f32[5,32,2,576]{3,1,2,0:T(8,128)}, u32[]{:S(2)}, u32[]{:S(2)}) collective-permute-start(f32[5,32,2,576]{3,1,2,0:T(8,128)} %get-tuple-element.23), channel_id=1, source_target_pairs={{0,2},{2,4},{4,6},{6,8},{8,10},{10,12},{12,14},{1,3},{3,5},{5,7},{... | collective-permute-start | bytes 2211848 | tf_op jit(solution)/shard_map/ppermute | solution.py:19
  18.7 24.3 %collective-permute-start.2 = (f32[5,32,4,2]{3,1,2,0:T(8,128)}, f32[5,32,4,2]{3,1,2,0:T(8,128)S(1)}, u32[]{:S(2)}, u32[]{:S(2)}) collective-permute-start(f32[5,32,4,2]{3,1,2,0:T(8,128)} %get-tuple-element.26), channel_id=1, source_target_pairs={{1,0},{0,1},{3,2},{2,3},{5,4},{4,5},{7,6},{6,7},{9,8},{8,9},{11,10... | collective-permute-start | bytes 15368 | tf_op jit(solution)/shard_map/ppermute | solution.py:22
  18.7 24.4 %collective-permute-start.3 = (f32[5,32,4,2]{3,1,2,0:T(8,128)S(1)}, f32[5,32,4,2]{3,1,2,0:T(8,128)}, u32[]{:S(2)}, u32[]{:S(2)}) collective-permute-start(f32[5,32,4,2]{3,1,2,0:T(8,128)S(1)} %get-tuple-element.27), channel_id=1, source_target_pairs={{0,1},{1,0},{2,3},{3,2},{4,5},{5,4},{6,7},{7,6},{8,9},{9,8},{10,11... | collective-permute-start | bytes 15368 | tf_op jit(solution)/shard_map/ppermute | solution.py:19
  19.7 22.7 %copy-start.6 = (pred[1152]{0:T(1024)(128)(4,1)}, pred[1152]{0:T(1024)(128)(4,1)S(1)}, u32[]{:S(2)}) copy-start(pred[1152]{0:T(1024)(128)(4,1)S(1)} %iota_compare_fusion.2) | copy-start | bytes 3460
  19.7 23.2 %copy-start.5 = (f32[4,4,576]{2,1,0:T(4,128)S(1)}, f32[4,4,576]{2,1,0:T(4,128)}, u32[]{:S(2)}) copy-start(f32[4,4,576]{2,1,0:T(4,128)} %param.13) | copy-start | bytes 110596
  45.6 7.4 %copy-start.10 = (f32[5]{0:T(128)S(1)}, f32[5]{0:T(128)}, u32[]{:S(2)}) copy-start(f32[5]{0:T(128)} %compare_convert_fusion) | copy-start | bytes 64
  53.0 1.3 copy-start.2
  56.9 3.4 %copy-start.9 = (f32[4,32]{1,0:T(4,128)S(1)}, f32[4,32]{1,0:T(4,128)}, u32[]{:S(2)}) copy-start(f32[4,32]{1,0:T(4,128)} %param.15) | copy-start | bytes 1540
  65.9 0.7 copy-start.11
  65.9 0.7 copy-start.8
  65.9 0.7 copy-start.7
  66.7 22.7 %copy-start.12 = (s32[1,1,18,1]{2,3,1,0:T(1,128)S(1)}, s32[1,1,18,1]{2,3,1,0:T(1,128)}, u32[]{:S(2)}) copy-start(s32[1,1,18,1]{2,3,1,0:T(1,128)} %param.16) | copy-start | bytes 220
  66.7 22.9 %copy-start.13 = (u32[32]{0:T(128)S(1)}, u32[32]{0:T(128)}, u32[]{:S(2)}) copy-start(u32[32]{0:T(128)} %constant.108) | copy-start | bytes 388
  111.9 22.8 %copy-start.1 = (f32[1152,1152]{1,0:T(8,128)S(1)}, f32[1152,1152]{1,0:T(8,128)}, u32[]{:S(2)}) copy-start(f32[1152,1152]{1,0:T(8,128)} %sine_select_fusion) | copy-start | bytes 15925252
Sparse Core Ops, SparseCore 0:
  66.1 23.0 all-gather.1
where the time goes:
time: 151 us
  other arithmetic  54.6 us (36%)
  matrix products  30.5 us (20%)
  blocking collectives  19.9 us (13%)
  between operations  16.1 us (11%)
  local copies, waits for them, and re-layouts  15.9 us (11%)
  starting transfers between devices  8.25 us (5%)
  waiting for transfers between devices  5.66 us (4%)
    dot_general x1, matrix products, on_device(): jnp.einsum('tkrx,xm->tkrm', lax.all_gather(physics_grid, 'lon', axis=3, t...  22.8 us
    select_n x1, other arithmetic, fourier_table(): return jnp.where(is_cosine, jnp.cos(radians), jnp.sin(radians))  22.6 us
    dot_general x1, other arithmetic, on_device(): jnp.einsum('tkrx,xm->tkrm', lax.all_gather(physics_grid, 'lon', axis=3, t...  22.6 us
    unnamed x1, blocking collectives  19.9 us
    ppermute x2, starting transfers between devices, padded_2(): lax.ppermute(lax.slice_in_dim(block, block.shape[dim] - width, None, axis...  6.93 us
    unnamed x34, local copies, waits for them, and re-layouts  6.68 us
    dot_general x1, matrix products, on_device(): jnp.einsum('tkrm,xm->tkrx', spectra * row_scale, own_table, precision=lax...  6.37 us
    ppermute x2, waiting for transfers between devices, padded_2(): lax.ppermute(lax.slice_in_dim(block, block.shape[dim] - width, None, axis...  5.61 us
  transfers between devices with their start and end apart: 5, of which 1 were waited for; matrix products, arithmetic and copies ran while one was open for 34% of the time, Pallas kernels for 0%

commit v1 on v0

v1 whole, which is shorter than its diff:
```python
import functools
import math

import jax
import jax.numpy as jnp
import numpy as np
from jax import lax
from jax.experimental import pallas as pl
from jax.experimental.pallas import tpu as pltpu
from jax.sharding import PartitionSpec as P

LANES = 128
BLOCK = 128
VMEM_BYTES = 24 * 1024 * 1024
NEAR = 7.0 / 12.0
FAR = 1.0 / 12.0
DOT_LAST = (((1,), (1,)), ((), ()))


def params():
    return pltpu.CompilerParams(vmem_limit_bytes=VMEM_BYTES)


def cost(flops, bytes_accessed):
    return pl.CostEstimate(flops=flops, bytes_accessed=bytes_accessed, transcendentals=0)


def split_high_low(value):
    high = value.astype(jnp.bfloat16)
    low = (value - high.astype(jnp.float32)).astype(jnp.bfloat16)
    return high, low


def split_table(table):
    high = table.astype(jnp.bfloat16.dtype)
    low = (table - high.astype(np.float64)).astype(jnp.bfloat16.dtype)
    return high, low


def spectral_tables(length):
    radix = length // LANES
    pairs = (radix - 1) // 2
    spot = np.arange(LANES)[:, None]
    number = np.arange(LANES)[None, :]
    is_cosine = number <= LANES // 2
    wave = np.where(is_cosine, number, number - LANES // 2)
    angle = 2.0 * np.pi * ((spot * wave) % LANES) / LANES
    first = np.where(is_cosine, np.cos(angle), np.sin(angle))
    others, numbers = [], [radix * wave[0]]
    weights = [np.where((wave[0] == 0) | (wave[0] == LANES // 2), 1.0, 2.0) / length]
    for residue in range(1, pairs + 1):
        whole = residue + radix * number
        angle = 2.0 * np.pi * ((spot * whole) % length) / length
        cosine, sine = np.cos(angle), np.sin(angle)
        others.append(np.block([[cosine, -sine], [sine, cosine]]))
        folded = np.minimum(whole[0], length - whole[0])
        numbers += [folded, folded]
        weights.append(np.full(2 * LANES, 2.0 / length))
    return first, np.concatenate(others, axis=0), np.concatenate(numbers), np.concatenate(weights)


def pack_rows(first, second):
    return jnp.concatenate([first, second], axis=1)


def second_half(packed, sector):
    skip, shift = sector // LANES, sector % LANES
    segments = [packed[:, LANES * i : LANES * (i + 1)] for i in range(packed.shape[1] // LANES)]
    if shift == 0:
        return jnp.concatenate(segments[skip:], axis=1)
    turned = [pltpu.roll(segment, LANES - shift, 1) for segment in segments[skip:]]
    lane = lax.broadcasted_iota(jnp.int32, turned[0].shape, 1)
    parts = [jnp.where(lane < LANES - shift, turned[i], turned[min(i + 1, len(turned) - 1)]) for i in range(len(turned))]
    return jnp.concatenate(parts, axis=1)


def pack_kernel(rows, levels, with_courant, *refs):
    if with_courant:
        tracer_ref, courant_ref, up_ref, down_ref = refs
    else:
        tracer_ref, up_ref, down_ref = refs
    up_ref[...] = pack_rows(tracer_ref[0, :, rows - 2, :], tracer_ref[0, :, rows - 1, :])
    down_ref[0:levels, :] = pack_rows(tracer_ref[0, :, 0, :], tracer_ref[0, :, 1, :])
    if with_courant:
        courant = courant_ref[:, 0, :]
        down_ref[levels : levels + levels // 2, :] = pack_rows(courant[: levels // 2], courant[levels // 2 :])


def base_kernel(rows, width, padded_ref, east_courant_ref, lat_courant_ref, base_ref):
    q = [padded_ref[0, r] for r in range(rows)]
    own_flux = [None] * (rows + 1)
    own_flux[0] = lat_courant_ref[0] * (NEAR * q[0] - FAR * q[1])
    own_flux[1] = lat_courant_ref[1] * (NEAR * (q[1] + q[0]) - FAR * q[2])
    own_flux[2] = lat_courant_ref[2] * (NEAR * (q[2] + q[1]) - FAR * (q[3] + q[0]))
    own_flux[3] = lat_courant_ref[3] * (NEAR * (q[3] + q[2]) - FAR * q[1])
    for r in range(rows):
        west, west2, east = pltpu.roll(q[r], 1, 1), pltpu.roll(q[r], 2, 1), pltpu.roll(q[r], width - 1, 1)
        flux = east_courant_ref[r] * (NEAR * (q[r] + west) - FAR * (east + west2))
        value = q[r] - (pltpu.roll(flux, width - 1, 1) - flux) + own_flux[r]
        if r + 1 < rows:
            value = value - own_flux[r + 1]
        base_ref[0, r] = value


def physics_kernel(rows, levels, sector, owner_count, *refs):
    if owner_count:
        owner_ref, refs = refs[0], refs[1:]
    (base_ref, padded_ref, low_ref, high_ref, courant_ref, top_ref, surface_ref, mixing_ref, decay_ref, energy_in_ref,
     physics_ref, energy_ref) = refs
    width = base_ref.shape[-1]
    low = low_ref[...]
    high = high_ref[0:levels, :]
    low_a, low_b = low[:, :width], second_half(low, sector)
    high_a, high_b = high[:, :width], second_half(high, sector)
    courant = [courant_ref[r] for r in range(rows)]
    south = courant[0] * (NEAR * low_b - FAR * low_a)
    south_in = courant[1] * (FAR * low_b)
    north_in = courant[3] * (FAR * high_a)
    north = top_ref[...] * (NEAR * (high_a + padded_ref[0, 3]) - FAR * (high_b + padded_ref[0, 2]))
    extra = [south + south_in, -south_in, north_in, -north_in - north]
    mix_high, mix_low = split_high_low(mixing_ref[...])
    mix = jnp.concatenate([mix_high, mix_high, mix_low, mix_low], axis=1)
    decay = decay_ref[0]
    level = lax.broadcasted_iota(jnp.int32, (levels, width), 0)
    lane = lax.broadcasted_iota(jnp.int32, (levels, width), 1)
    energies = []
    for r in range(rows):
        advected = base_ref[0, r] + extra[r]
        part_high, part_low = split_high_low(advected)
        stacked = jnp.concatenate([part_high, part_low, part_high, part_low], axis=0)
        mixed = jnp.dot(mix, stacked, preferred_element_type=jnp.float32)
        mixed = jnp.where(level == levels - 1, mixed + surface_ref[0, r : r + 1, :], mixed)
        physics = mixed / (1.0 + decay * mixed * mixed)
        physics_ref[r] = physics
        gap = jnp.where(lane < sector, physics - advected, 0.0)
        squared = gap * gap
        total = energy_in_ref[r]
        for k in range(levels // 8):
            total = total + squared[8 * k : 8 * k + 8]
        energies.append(total)
    if not owner_count:
        for r in range(rows):
            energy_ref[r] = energies[r]
        return
    spot = lax.broadcasted_iota(jnp.int32, (1, LANES), 1)
    result = jnp.zeros((1, LANES), jnp.float32)
    for owner in range(owner_count):
        chosen = jnp.zeros((8, LANES), jnp.float32)
        for r in range(rows):
            picked = jnp.where(owner_ref[r : r + 1, :] == owner, energies[r], 0.0)
            for k in range(width // LANES):
                chosen = chosen + picked[:, LANES * k : LANES * (k + 1)]
        summed = jnp.sum(jnp.sum(chosen, axis=0, keepdims=True), axis=1, keepdims=True)
        result = jnp.where(spot == owner, summed, result)
    energy_ref[...] = result


def filter_kernel(rows, levels, sector, radix, has_alias, *refs):
    mask_ref, own_ref, other_ref, table_high_ref, table_low_ref, first_high_ref, first_low_ref, scale_ref = refs[:8]
    out_ref, high_ref, low_ref, wave_ref = refs[8 + has_alias :]
    pairs = (radix - 1) // 2
    shift = sector % LANES
    own_segments = -(-sector // LANES)
    lane = lax.broadcasted_iota(jnp.int32, (levels, LANES), 1)
    cosine = lambda k, i: math.cos(2.0 * math.pi * ((k * i) % radix) / radix)
    sine = lambda k, i: math.sin(2.0 * math.pi * ((k * i) % radix) / radix)

    for r in range(rows):
        own = [own_ref[r, :, LANES * i : LANES * (i + 1)] for i in range(own_segments)]
        turned = [pltpu.roll(other_ref[r, :, LANES * i : LANES * (i + 1)], shift, 1) for i in range(own_segments)]
        joined = own[:-1] + [jnp.where(lane < shift, own[-1], turned[0])]
        joined += [jnp.where(lane < shift, turned[i], turned[i + 1]) for i in range(own_segments - 1)]
        plus = [joined[i] + joined[radix - i] for i in range(1, pairs + 1)]
        minus = [joined[radix - i] - joined[i] for i in range(1, pairs + 1)]
        waves = [sum(plus, joined[0])]
        for k in range(1, pairs + 1):
            waves.append(sum((cosine(k, i) * plus[i - 1] for i in range(1, pairs + 1)), joined[0]))
            waves.append(sum(sine(k, i) * minus[i - 1] for i in range(1, pairs + 1)))
        for i, wave in enumerate(waves):
            part_high, part_low = split_high_low(wave)
            high_ref[levels * r : levels * (r + 1), LANES * i : LANES * (i + 1)] = part_high
            low_ref[levels * r : levels * (r + 1), LANES * i : LANES * (i + 1)] = part_low

    def both_ways(begin, size, table_high, table_low):
        count = rows * levels

        def product(part_high, part_low, dims):
            stacked = jnp.concatenate([part_high, part_low], axis=0)
            main = lax.dot_general(stacked, table_high, dims, preferred_element_type=jnp.float32)
            rest = lax.dot_general(part_high, table_low, dims, preferred_element_type=jnp.float32)
            return main[:count] + (main[count:] + rest)

        spectrum = product(high_ref[:, begin : begin + size], low_ref[:, begin : begin + size], (((1,), (0,)), ((), ())))
        scaled = jnp.concatenate(
            [spectrum[levels * r : levels * (r + 1)] * scale_ref[r : r + 1, begin : begin + size] for r in range(rows)], axis=0
        )
        wave_ref[:, begin : begin + size] = product(*split_high_low(scaled), DOT_LAST)

    both_ways(0, LANES, first_high_ref[...], first_low_ref[...])
    for k in range(pairs):
        both_ways(
            LANES * (2 * k + 1), 2 * LANES,
            table_high_ref[2 * LANES * k : 2 * LANES * (k + 1), :], table_low_ref[2 * LANES * k : 2 * LANES * (k + 1), :],
        )

    for r in range(rows):
        waves = [wave_ref[levels * r : levels * (r + 1), LANES * i : LANES * (i + 1)] for i in range(radix)]
        filtered_row = mask_ref[r] == 1
        for n in range(own_segments):
            value = waves[0]
            for k in range(1, pairs + 1):
                value = value + cosine(k, n) * waves[2 * k - 1]
                if n:
                    value = value - sine(k, n) * waves[2 * k]
            begin = LANES * n
            size = min(LANES, sector - begin)
            value = jnp.where(filtered_row, value, own_ref[r, :, begin : begin + LANES])
            out_ref[0, :, r, begin : begin + size] = value[:, :size]


def vmem(shape, index=None):
    index = index or (0,) * len(shape)
    return pl.BlockSpec(shape, lambda i: index)


def on_device(tracers, courant_lat, courant_lon, surface_flux, mixing, decay_rate, owners, polar_mask):
    tracer_count, levels, rows, sector = tracers.shape
    assert rows == 4 and sector % 64 == 0 and lax.axis_size("lon") == 2
    f32 = jnp.float32
    lat_count, lat = lax.axis_size("lat"), lax.axis_index("lat")
    length = 2 * sector
    width = -(-sector // LANES) * LANES
    radix = length // LANES
    upward = [(i, i + 1) for i in range(lat_count - 1)]
    downward = [(i + 1, i) for i in range(lat_count - 1)]
    swap = [(0, 1), (1, 0)]

    from_south, from_north = [], []
    for t in range(tracer_count):
        with_courant = t == 0
        down_rows = levels + (levels // 2 if with_courant else 0)
        up, down = pl.pallas_call(
            functools.partial(pack_kernel, rows, levels, with_courant),
            grid=(1,),
            in_specs=[vmem((1, levels, rows, sector), (t, 0, 0, 0))]
            + ([vmem((levels, rows, sector))] if with_courant else []),
            out_specs=[vmem((levels, length)), vmem((down_rows, length))],
            out_shape=[jax.ShapeDtypeStruct((levels, length), f32), jax.ShapeDtypeStruct((down_rows, length), f32)],
            compiler_params=params(),
            cost_estimate=cost(0, 600_000),
            name="pack",
        )(tracers, *([courant_lat] if with_courant else []))
        from_south.append(lax.ppermute(up, "lat", upward))
        from_north.append(lax.ppermute(down, "lat", downward))

    by_row = jnp.transpose(tracers, (0, 2, 1, 3))
    lon_by_row = jnp.transpose(courant_lon, (1, 0, 2))
    lat_by_row = jnp.transpose(courant_lat, (1, 0, 2))
    ends = jnp.concatenate([by_row[..., -2:], by_row[..., :2]], axis=-1)
    lon_end = jnp.pad(lon_by_row[..., :1], ((0, 0), (0, 0), (0, 3)))
    sides = lax.ppermute(jnp.concatenate([ends, lon_end[None]], axis=0), "lon", swap)
    gap = width - sector - 4
    padded = jnp.concatenate(
        [by_row, sides[:tracer_count, ..., 2:], jnp.zeros((tracer_count, rows, levels, gap), f32), sides[:tracer_count, ..., :2]],
        axis=-1,
    )
    east_courant = jnp.concatenate(
        [lon_by_row, sides[tracer_count, ..., :1], jnp.zeros((rows, levels, width - sector - 1), f32)], axis=-1
    )
    not_pole = jnp.where((lat > 0) | (jnp.arange(rows) > 0), 1.0, 0.0)
    lat_courant = jnp.pad(lat_by_row * not_pole[:, None, None], ((0, 0), (0, 0), (0, width - sector)))
    base = pl.pallas_call(
        functools.partial(base_kernel, rows, width),
        grid=(tracer_count,),
        in_specs=[
            pl.BlockSpec((1, rows, levels, width), lambda t: (t, 0, 0, 0)),
            vmem((rows, levels, width)),
            vmem((rows, levels, width)),
        ],
        out_specs=pl.BlockSpec((1, rows, levels, width), lambda t: (t, 0, 0, 0)),
        out_shape=jax.ShapeDtypeStruct((tracer_count, rows, levels, width), f32),
        compiler_params=params(),
        cost_estimate=cost(0, 3_000_000),
        name="base",
    )(padded, east_courant, lat_courant)

    surface = jnp.pad(surface_flux, ((0, 0), (0, 0), (0, width - sector)))
    decay = decay_rate[:, :, None]
    block_count = rows * sector // BLOCK
    block_of = (np.arange(rows)[:, None] * sector + np.minimum(np.arange(width), sector - 1)[None]) // BLOCK
    owner_of = jnp.repeat(owners.reshape(block_count), BLOCK).reshape(rows, sector)
    owner_of = jnp.pad(owner_of, ((0, 0), (0, width - sector)))
    first, others, numbers, weights = spectral_tables(length)
    first_high, first_low = split_table(first)
    others_high, others_low = split_table(others)
    row_ids = (lat * rows + jnp.arange(rows)).astype(f32)
    latitude = (-0.5 + (row_ids + 0.5) / (lat_count * rows)) * math.pi
    inverse_sine = np.where(numbers == 0, 1.0, 1.0 / np.where(numbers == 0, 1.0, np.sin(np.pi * numbers / length)))
    ratio = 2.0 * jnp.cos(latitude)[:, None] * jnp.asarray(inverse_sine, f32)[None]
    damping = jnp.where(jnp.asarray(numbers == 0)[None], 1.0, jnp.minimum(1.0, ratio * ratio))
    scale = damping * jnp.asarray(weights, f32)[None]

    top_packed = from_north[0][levels:]
    top = jnp.concatenate([top_packed[:, :sector], top_packed[:, sector:]], axis=0)
    top = jnp.pad(top, ((0, 0), (0, width - sector)))

    energy = jnp.zeros((rows, 8, width), f32)
    own_parts, other_parts = [], []
    for t in range(tracer_count):
        last = t == tracer_count - 1
        energy_shape = (1, LANES) if last else (rows, 8, width)
        down_rows = from_north[t].shape[0]
        physics, energy = pl.pallas_call(
            functools.partial(physics_kernel, rows, levels, sector, lat_count if last else 0),
            grid=(1,),
            in_specs=([vmem((rows, width))] if last else [])
            + [
                vmem((1, rows, levels, width), (t, 0, 0, 0)),
                vmem((1, rows, levels, width), (t, 0, 0, 0)),
                vmem((levels, length)),
                vmem((down_rows, length)),
                vmem((rows, levels, width)),
                vmem((levels, width)),
                vmem((1, rows, width), (t, 0, 0)),
                vmem((levels, levels)),
                vmem((1, levels, 1), (t, 0, 0)),
                vmem((rows, 8, width)),
            ],
            out_specs=[vmem((rows, levels, width)), vmem(energy_shape)],
            out_shape=[jax.ShapeDtypeStruct((rows, levels, width), f32), jax.ShapeDtypeStruct(energy_shape, f32)],
            compiler_params=params(),
            cost_estimate=cost(50_000_000, 2_000_000),
            name="physics",
        )(
            *([owner_of] if last else []),
            base, padded, from_south[t], from_north[t], lat_courant, top, surface, mixing, decay, energy,
        )
        own_parts.append(physics)
        other_parts.append(lax.ppermute(physics, "lon", swap))

    out = None
    tables = (others_high, others_low, first_high, first_low)
    for t in range(tracer_count):
        has_alias = int(out is not None)
        out = pl.pallas_call(
            functools.partial(filter_kernel, rows, levels, sector, radix, has_alias),
            grid=(1,),
            in_specs=[
                pl.BlockSpec(memory_space=pltpu.SMEM),
                vmem((rows, levels, width)),
                vmem((rows, levels, width)),
                vmem(others_high.shape),
                vmem(others_low.shape),
                vmem(first_high.shape),
                vmem(first_low.shape),
                vmem((rows, length)),
            ]
            + [pl.BlockSpec(memory_space=pl.ANY)] * has_alias,
            out_specs=vmem((1, levels, rows, sector), (t, 0, 0, 0)),
            out_shape=jax.ShapeDtypeStruct(tracers.shape, f32),
            scratch_shapes=[
                pltpu.VMEM((rows * levels, length), jnp.bfloat16),
                pltpu.VMEM((rows * levels, length), jnp.bfloat16),
                pltpu.VMEM((rows * levels, length), f32),
            ],
            input_output_aliases={8: 0} if has_alias else {},
            compiler_params=params(),
            cost_estimate=cost(450_000_000, 3_000_000),
            name="filter",
        )(polar_mask, own_parts[t], other_parts[t], *(jnp.asarray(table) for table in tables), scale, *([out] if has_alias else []))

    step = 1
    while step < lat_count:
        energy = energy + lax.ppermute(energy, "lat", [(i, i ^ step) for i in range(lat_count)])
        step *= 2
    owner_energy = lax.dynamic_slice(energy, (0, lat), (1, 1)) / (block_count * BLOCK)
    return out, owner_energy


def solution(mesh):
    placed = (
        P("group", None, "lat", "lon"),
        P("group", "lat", "lon"),
        P("group", "lat", "lon"),
        P("group", "lat", "lon"),
        P(),
        P(),
        P(("group", "lat"), "lon", None, None),
        P(("group", "lat")),
    )
    return jax.shard_map(
        on_device,
        mesh=mesh,
        in_specs=placed,
        out_specs=(P("group", None, "lat", "lon"), P(("group", "lat"), "lon")),
        check_vma=False,
    )
```

time: 151 us -> 69.6 us (0.46)
  other arithmetic: 54.6 us -> 3.41 us
  matrix products: 30.5 us -> 0 us
  starting transfers between devices: 8.25 us -> 32.9 us
  blocking collectives: 19.9 us -> 0 us
  Pallas kernels: 0 us -> 17.2 us
  between operations: 16.1 us -> 1.06 us
  local copies, waits for them, and re-layouts: 15.9 us -> 5.36 us
  waiting for transfers between devices: 5.66 us -> 9.09 us
    dot_general x4 -> x0, matrix products: 30.5 us -> none  [the longest x1 22.8 us: on_device(): jnp.einsum('tkrx,xm->tkrm', lax.all_gather(physics_grid, 'lon', axis=3, t...]
    ppermute x4 -> x16, starting transfers between devices: 8.21 us -> 32.9 us  [the longest x4 19.1 us: on_device(): from_south.append(lax.ppermute(up, 'lat', upward))]
    select_n x3 -> x1, other arithmetic: 22.7 us -> 0.01 us  [on_device(): not_pole = jnp.where((lat > 0) | (jnp.arange(rows) > 0), 1.0, 0.0)]
    dot_general x1 -> x0, other arithmetic: 22.6 us -> none  [on_device(): jnp.einsum('tkrx,xm->tkrm', lax.all_gather(physics_grid, 'lon', axis=3, t...]
    unnamed x1 -> x0, blocking collectives: 19.9 us -> none
    pallas_call x0 -> x13, Pallas kernels: none -> 17.2 us  [the longest x4 11.9 us: on_device(): pl.pallas_call(functools.partial(filter_kernel, rows, levels, sector, rad...]
    reshape x4 -> x0, local copies, waits for them, and re-layouts: 5.56 us -> none  [the longest x2 4.34 us: on_device(): physics_blocks.transpose(1, 2, 0, 3)]
    unnamed x34 -> x40, local copies, waits for them, and re-layouts: 6.68 us -> 2.68 us
  transfers between devices with their start and end apart: 5 -> 16, of which waited for: 1 -> 5; matrix products, arithmetic and copies ran while one was open for 34% -> 7% of each run, Pallas kernels for 0% -> 20%
where the time goes in v1:
time: 69.6 us; the launch traced here: 69 us
  starting transfers between devices  32.9 us (47%)
  Pallas kernels  17.2 us (25%)
  waiting for transfers between devices  9.09 us (13%)
  local copies, waits for them, and re-layouts  5.36 us (8%)
  other arithmetic  3.41 us (5%)
  between operations  1.06 us (2%)
    ppermute x4, starting transfers between devices, on_device(): from_south.append(lax.ppermute(up, 'lat', upward))  19.1 us
    pallas_call x4, Pallas kernels, on_device(): pl.pallas_call(functools.partial(filter_kernel, rows, levels, sector, rad...  11.9 us
    ppermute x3, starting transfers between devices, on_device(): lax.ppermute(energy, 'lat', [(i, i ^ step) for i in range(lat_count)])  7.09 us
    ppermute x4, starting transfers between devices, on_device(): from_north.append(lax.ppermute(down, 'lat', downward))  5.17 us
    ppermute x3, waiting for transfers between devices, on_device(): lax.ppermute(energy, 'lat', [(i, i ^ step) for i in range(lat_count)])  4.1 us
    ppermute x4, waiting for transfers between devices, on_device(): from_south.append(lax.ppermute(up, 'lat', upward))  3.16 us
    unnamed x40, local copies, waits for them, and re-layouts  2.68 us
    pallas_call x1, Pallas kernels, on_device(): pl.pallas_call(functools.partial(base_kernel, rows, width), grid=(tracer_...  2.6 us
  transfers between devices with their start and end apart: 16, of which 5 were waited for; matrix products, arithmetic and copies ran while one was open for 7% of the time, Pallas kernels for 20%

profile of v1, /device:TPU:0, one launch (start us, length us, event | category | flops | bytes accessed | tf_op | source)
XLA Modules:
  0.0 69.0 jit_solution(15266155514691844628)
XLA Ops:
  0.6 1.5 %copy.72 = f32[4,32,4,576]{3,1,2,0:T(8,128)S(1)} copy(f32[4,32,4,576]{3,2,1,0:T(4,128)} %refs_0_.11) | data formatting | bytes 2359296 | tf_op args[0]
  2.1 0.0 copy-start.8
  2.2 0.0 copy-start.17
  2.2 0.0 copy-start
  2.2 0.0 copy-start.3
  2.2 0.1 fusion.2
  2.4 0.7 %copy-done.9 = f32[32,4,576]{2,0,1:T(8,128)} copy-done((f32[32,4,576]{2,0,1:T(8,128)}, f32[32,4,576]{2,0,1:T(8,128)S(1)}, u32[]{:S(2)}) %copy-start.9) | copy-done | bytes 294936
  3.1 0.9 %pad_maximum_fusion.1 = f32[5,4,32,4]{3,2,1,0:T(8,128)} fusion(f32[1,4,32,4]{3,2,1,0:T(8,128)S(1)} %fusion.1, f32[4,4,32,2]{3,2,1,0:T(8,128)S(1)} %get-tuple-element.35, f32[4,4,32,2]{3,2,1,0:T(8,128)S(1)} %get-tuple-element.34), kind=kLoop, calls=%fused_computation.2 | loop fusion | flops 5120 | bytes 20480 | tf_op jit(solution)/shard_map/concatenate | solution.py:261
  4.0 0.5 collective-permute-start
  4.4 0.1 pack.5
  4.6 1.3 %collective-permute-start.3 = (f32[48,1152]{1,0:T(8,128)S(1)}, f32[48,1152]{1,0:T(8,128)S(1)}, u32[]{:S(2)}, u32[]{:S(2)}) collective-permute-start(f32[48,1152]{1,0:T(8,128)S(1)} %get-tuple-element.20), channel_id=1, source_target_pairs={{2,0},{4,2},{6,4},{8,6},{10,8},{12,10},{14,12},{3,1},{5,3},{7,5},{... | collective-permute-start | bytes 663560 | tf_op jit(solution)/shard_map/ppermute | solution.py:254
  5.9 5.2 %collective-permute-start.8 = (f32[32,1152]{1,0:T(8,128)S(1)}, f32[32,1152]{1,0:T(8,128)S(1)}, u32[]{:S(2)}, u32[]{:S(2)}) collective-permute-start(f32[32,1152]{1,0:T(8,128)S(1)} %get-tuple-element.25), channel_id=1, source_target_pairs={{0,2},{2,4},{4,6},{6,8},{8,10},{10,12},{12,14},{1,3},{3,5},{5,7},{... | collective-permute-start | bytes 442376 | tf_op jit(solution)/shard_map/ppermute | solution.py:253
  11.1 0.1 pack.7
  11.2 4.8 %collective-permute-start.6 = (f32[32,1152]{1,0:T(8,128)S(1)}, f32[32,1152]{1,0:T(8,128)S(1)}, u32[]{:S(2)}, u32[]{:S(2)}) collective-permute-start(f32[32,1152]{1,0:T(8,128)S(1)} %get-tuple-element.23), channel_id=1, source_target_pairs={{0,2},{2,4},{4,6},{6,8},{8,10},{10,12},{12,14},{1,3},{3,5},{5,7},{... | collective-permute-start | bytes 442376 | tf_op jit(solution)/shard_map/ppermute | solution.py:253
  16.0 1.3 %collective-permute-start.7 = (f32[32,1152]{1,0:T(8,128)S(1)}, f32[32,1152]{1,0:T(8,128)S(1)}, u32[]{:S(2)}, u32[]{:S(2)}) collective-permute-start(f32[32,1152]{1,0:T(8,128)S(1)} %get-tuple-element.24), channel_id=1, source_target_pairs={{2,0},{4,2},{6,4},{8,6},{10,8},{12,10},{14,12},{3,1},{5,3},{7,5},{... | collective-permute-start | bytes 442376 | tf_op jit(solution)/shard_map/ppermute | solution.py:254
  17.3 0.1 fusion
  17.4 0.8 %pack.6 = (f32[32,1152]{1,0:T(8,128)}, f32[32,1152]{1,0:T(8,128)}) custom-call(f32[4,32,4,576]{3,2,1,0:T(4,128)S(1)} %copy-done), custom_call_target="tpu_custom_call" | custom-call | bytes 600000 | tf_op jit(solution)/shard_map/pack/pallas_call | solution.py:242
  18.2 0.1 pack.4
  18.4 0.1 pad.32.clone
  18.5 0.1 pad.29.clone
  18.6 0.4 copy-done.15
  18.9 0.1 copy.66.refs_8_.refs_9_
  19.0 0.0 copy-done.12
  19.1 0.1 broadcast_in_dim.43
  19.1 0.1 reshape_reshape.3
  19.2 0.0 collective-permute-done
  19.2 4.6 %collective-permute-start.4 = (f32[32,1152]{1,0:T(8,128)}, f32[32,1152]{1,0:T(8,128)S(1)}, u32[]{:S(2)}, u32[]{:S(2)}) collective-permute-start(f32[32,1152]{1,0:T(8,128)} %get-tuple-element.21), channel_id=1, source_target_pairs={{0,2},{2,4},{4,6},{6,8},{8,10},{10,12},{12,14},{1,3},{3,5},{5,7},{... | collective-permute-start | bytes 442376 | tf_op jit(solution)/shard_map/ppermute | solution.py:253
  23.8 1.2 %fusion.3 = (f32[4,4,32,2]{3,2,1,0:T(8,128)S(1)}, f32[4,4,32,2]{3,2,1,0:T(8,128)S(1)}) fusion(f32[5,4,32,4]{3,2,1,0:T(8,128)} %collective-permute-done), kind=kLoop, calls=%fused_computation.17 | loop fusion | bytes 16384 | tf_op jit(solution)/shard_map/slice | solution.py:264
  25.0 1.6 %pad_maximum_fusion.padded_ref.refs_1_.refs_2_ = f32[4,4,32,640]{3,2,1,0:T(8,128)S(1)} fusion(f32[4,4,32,2]{3,2,1,0:T(8,128)S(1)} %get-tuple-element.37, f32[4,4,32,2]{3,2,1,0:T(8,128)S(1)} %get-tuple-element.36, f32[4,4,32,576]{3,2,1,0:T(8,128)} %bitcast.15, f32[640]{0:T(1024)S(1)} %pad.32.clone), kind=kLoop, calls=%fused_computation | loop fusion | flops 983040 | bytes 2501120 | tf_op jit(solution)/shard_map/concatenate | solution.py:263
  26.6 0.8 %slice_bitcast_fusion = f32[4,32,1]{2,1,0:T(8,128)S(1)} fusion(f32[5,4,32,4]{3,2,1,0:T(8,128)} %collective-permute-done), kind=kLoop, calls=%fused_computation.9 | loop fusion | bytes 1024 | tf_op jit(solution)/shard_map/squeeze | solution.py:268
  27.4 0.1 maximum_maximum_fusion.east_courant_ref
  27.5 0.0 copy-start.6
  27.5 2.6 %base.1.refs_0_.refs_1_ = f32[4,4,32,640]{3,2,1,0:T(8,128)S(1)} custom-call(f32[4,4,32,640]{3,2,1,0:T(8,128)S(1)} %pad_maximum_fusion.padded_ref.refs_1_.refs_2_, f32[4,32,640]{2,1,0:T(8,128)S(1)} %maximum_maximum_fusion.east_courant_ref, f32[4,32,640]{2,1,0:T(8,128)S(1)} %pad.22.lat_courant_ref.refs_4_.refs_5_), custom_call_target="tpu_custom_call" | custom-call | bytes 3000000 | tf_op jit(solution)/shard_map/base/pallas_call | solution.py:272
  30.2 1.3 %collective-permute-start.5 = (f32[32,1152]{1,0:T(8,128)}, f32[32,1152]{1,0:T(8,128)S(1)}, u32[]{:S(2)}, u32[]{:S(2)}) collective-permute-start(f32[32,1152]{1,0:T(8,128)} %get-tuple-element.22), channel_id=1, source_target_pairs={{2,0},{4,2},{6,4},{8,6},{10,8},{12,10},{14,12},{3,1},{5,3},{7,5},{... | collective-permute-start | bytes 442376 | tf_op jit(solution)/shard_map/ppermute | solution.py:254
  31.5 0.0 collective-permute-done.6.refs_2_
  31.5 4.6 %collective-permute-start.1 = (f32[32,1152]{1,0:T(8,128)S(1)}, f32[32,1152]{1,0:T(8,128)S(1)}, u32[]{:S(2)}, u32[]{:S(2)}) collective-permute-start(f32[32,1152]{1,0:T(8,128)S(1)} %get-tuple-element.18), channel_id=1, source_target_pairs={{0,2},{2,4},{4,6},{6,8},{8,10},{10,12},{12,14},{1,3},{3,5},{5,7},{... | collective-permute-start | bytes 442376 | tf_op jit(solution)/shard_map/ppermute | solution.py:253
  36.0 1.3 %collective-permute-start.2 = (f32[32,1152]{1,0:T(8,128)S(1)}, f32[32,1152]{1,0:T(8,128)S(1)}, u32[]{:S(2)}, u32[]{:S(2)}) collective-permute-start(f32[32,1152]{1,0:T(8,128)S(1)} %get-tuple-element.19), channel_id=1, source_target_pairs={{2,0},{4,2},{6,4},{8,6},{10,8},{12,10},{14,12},{3,1},{5,3},{7,5},{... | collective-permute-start | bytes 442376 | tf_op jit(solution)/shard_map/ppermute | solution.py:254
  37.3 0.1 fusion.4
  37.5 0.3 physics.4
  37.8 0.3 physics.5
  38.2 0.3 physics.6
  38.6 3.1 %collective-permute-done.1.refs_3_ = f32[32,1152]{1,0:T(8,128)S(1)} collective-permute-done((f32[32,1152]{1,0:T(8,128)S(1)}, f32[32,1152]{1,0:T(8,128)S(1)}, u32[]{:S(2)}, u32[]{:S(2)}) %collective-permute-start.1) | collective-permute-done | bytes 147488 | tf_op jit(solution)/shard_map/ppermute | solution.py:253
  41.7 1.8 %collective-permute-done.2.refs_4_ = f32[32,1152]{1,0:T(8,128)S(1)} collective-permute-done((f32[32,1152]{1,0:T(8,128)S(1)}, f32[32,1152]{1,0:T(8,128)S(1)}, u32[]{:S(2)}, u32[]{:S(2)}) %collective-permute-start.2) | collective-permute-done | bytes 147488 | tf_op jit(solution)/shard_map/ppermute | solution.py:254
  43.5 0.0 copy-start.2
  43.5 0.0 copy-start.4
  43.5 0.0 copy-start.5
  43.6 0.0 copy-start.7
  43.6 0.5 physics.7
  44.1 2.9 %collective-permute-start.13 = (f32[1,128]{1,0:T(1,128)S(1)}, f32[1,128]{1,0:T(1,128)S(1)}, u32[]{:S(2)}, u32[]{:S(2)}) collective-permute-start(f32[1,128]{1,0:T(1,128)S(1)} %get-tuple-element.33), channel_id=1, source_target_pairs={{0,2},{2,0},{4,6},{6,4},{8,10},{10,8},{12,14},{14,12},{1,3},{3,1},... | collective-permute-start | bytes 1544 | tf_op jit(solution)/shard_map/ppermute | solution.py:374
  47.0 1.5 %collective-permute-done.13 = f32[1,128]{1,0:T(1,128)S(1)} collective-permute-done((f32[1,128]{1,0:T(1,128)S(1)}, f32[1,128]{1,0:T(1,128)S(1)}, u32[]{:S(2)}, u32[]{:S(2)}) %collective-permute-start.13) | collective-permute-done | bytes 544 | tf_op jit(solution)/shard_map/ppermute | solution.py:374
  48.5 1.6 %collective-permute-start.14 = (f32[1,128]{1,0:T(1,128)S(1)}, f32[1,128]{1,0:T(1,128)S(1)}, u32[]{:S(2)}, u32[]{:S(2)}) collective-permute-start(f32[1,128]{1,0:T(1,128)S(1)} %add.48), channel_id=1, source_target_pairs={{0,4},{2,6},{4,0},{6,2},{8,12},{10,14},{12,8},{14,10},{1,5},{3,7},... | collective-permute-start | bytes 1544 | tf_op jit(solution)/shard_map/ppermute | solution.py:374
  50.2 0.1 collective-permute-start.12
  50.2 0.5 collective-permute-start.11
  50.7 0.1 collective-permute-start.10
  50.8 0.4 collective-permute-start.9
  51.2 0.8 %collective-permute-done.14 = f32[1,128]{1,0:T(1,128)S(1)} collective-permute-done((f32[1,128]{1,0:T(1,128)S(1)}, f32[1,128]{1,0:T(1,128)S(1)}, u32[]{:S(2)}, u32[]{:S(2)}) %collective-permute-start.14) | collective-permute-done | bytes 544 | tf_op jit(solution)/shard_map/ppermute | solution.py:374
  52.1 2.6 %collective-permute-start.15 = (f32[1,128]{1,0:T(1,128)S(1)}, f32[1,128]{1,0:T(1,128)S(1)}, u32[]{:S(2)}, u32[]{:S(2)}) collective-permute-start(f32[1,128]{1,0:T(1,128)S(1)} %add.49), channel_id=1, source_target_pairs={{0,8},{2,10},{4,12},{6,14},{8,0},{10,2},{12,4},{14,6},{1,9},{3,11}... | collective-permute-start | bytes 1544 | tf_op jit(solution)/shard_map/ppermute | solution.py:374
  54.7 0.1 select_multiply_fusion.refs_7_
  54.8 1.8 %collective-permute-done.15 = f32[1,128]{1,0:T(1,128)S(1)} collective-permute-done((f32[1,128]{1,0:T(1,128)S(1)}, f32[1,128]{1,0:T(1,128)S(1)}, u32[]{:S(2)}, u32[]{:S(2)}) %collective-permute-start.15) | collective-permute-done | bytes 544 | tf_op jit(solution)/shard_map/ppermute | solution.py:374
  56.5 0.6 fusion.5
  57.1 3.3 %filter.4.refs_8_ = f32[4,32,4,576]{3,2,1,0:T(4,128)} custom-call(s32[4]{0:T(128)S(1)} %copy-done.7, f32[4,32,640]{2,1,0:T(8,128)S(1)} %get-tuple-element.32.refs_1_, f32[4,32,640]{2,1,0:T(8,128)} %collective-permute-done.12.refs_2_, bf16[1024,256]{1,0:T(8,128)(2,1)S(1)} %copy-done.1, bf16[1024,256]{1,0:T(8,128)(2,1)S(1)} %copy-done.2, ...), custom_call_target="tpu_custom_call" | custom-call | flops 450000000 | bytes 3000000 | tf_op jit(solution)/shard_map/filter/pallas_call | solution.py:345
  60.4 2.9 %filter.5.refs_8_ = f32[4,32,4,576]{3,2,1,0:T(4,128)} custom-call(s32[4]{0:T(128)S(1)} %copy-done.7, f32[4,32,640]{2,1,0:T(8,128)S(1)} %get-tuple-element.31.refs_1_, f32[4,32,640]{2,1,0:T(8,128)S(1)} %collective-permute-done.11.refs_2_, bf16[1024,256]{1,0:T(8,128)(2,1)S(1)} %copy-done.1, ...), custom_call_target="tpu_custom_call", output_to_operand_aliasing={{}: (8, {})} | custom-call | flops 450000000 | bytes 3000000 | tf_op jit(solution)/shard_map/filter/pallas_call | solution.py:345
  63.3 2.9 %filter.6.refs_8_ = f32[4,32,4,576]{3,2,1,0:T(4,128)} custom-call(s32[4]{0:T(128)S(1)} %copy-done.7, f32[4,32,640]{2,1,0:T(8,128)S(1)} %get-tuple-element.30.refs_1_, f32[4,32,640]{2,1,0:T(8,128)S(1)} %collective-permute-done.10.refs_2_, bf16[1024,256]{1,0:T(8,128)(2,1)S(1)} %copy-done.1, ...), custom_call_target="tpu_custom_call", output_to_operand_aliasing={{}: (8, {})} | custom-call | flops 450000000 | bytes 3000000 | tf_op jit(solution)/shard_map/filter/pallas_call | solution.py:345
  66.2 2.9 %filter.7 = f32[4,32,4,576]{3,2,1,0:T(4,128)} custom-call(s32[4]{0:T(128)S(1)} %copy-done.7, f32[4,32,640]{2,1,0:T(8,128)S(1)} %get-tuple-element.29.refs_1_, f32[4,32,640]{2,1,0:T(8,128)S(1)} %collective-permute-done.9.refs_2_, bf16[1024,256]{1,0:T(8,128)(2,1)S(1)} %copy-done.1, bf16[1024,256]{1,0:T(8,128)(2,1)S(1)} %copy-done.2, ...), custom_call_target="tpu_custom_call", output_to_operand_aliasing={{}: (8, {})} | custom-call | flops 450000000 | bytes 3000000 | tf_op jit(solution)/shard_map/filter/pallas_call | solution.py:345
  (49 shorter events, 0.2 us)
Async XLA Ops:
  0.6 1.7 %copy-start.11 = (f32[32,4,576]{2,1,0:T(4,128)S(1)}, f32[32,4,576]{2,1,0:T(4,128)}, u32[]{:S(2)}) copy-start(f32[32,4,576]{2,1,0:T(4,128)} %param.17) | copy-start | bytes 884740
  2.1 1.8 %copy-start.8 = (f32[4,32,4,576]{3,1,2,0:T(8,128)}, f32[4,32,4,576]{3,1,2,0:T(8,128)S(1)}, u32[]{:S(2)}) copy-start(f32[4,32,4,576]{3,1,2,0:T(8,128)S(1)} %copy.72) | copy-start | bytes 3538948
  2.2 0.9 %copy-start.17 = (pred[4]{0:T(512)(128)(4,1)S(1)}, pred[4]{0:T(512)(128)(4,1)}, u32[]{:S(2)}) copy-start(pred[4]{0:T(512)(128)(4,1)} %constant.22.clone.1) | copy-start | bytes 16
  2.2 2.3 %copy-start = (f32[4,32,4,576]{3,2,1,0:T(4,128)S(1)}, f32[4,32,4,576]{3,2,1,0:T(4,128)}, u32[]{:S(2)}) copy-start(f32[4,32,4,576]{3,2,1,0:T(4,128)} %refs_0_.11) | copy-start | bytes 3538948
  2.2 2.2 %copy-start.3 = (f32[32,4,576]{2,1,0:T(4,128)S(1)}, f32[32,4,576]{2,1,0:T(4,128)}, u32[]{:S(2)}) copy-start(f32[32,4,576]{2,1,0:T(4,128)} %refs_1_.1) | copy-start | bytes 884740
  2.4 0.7 %copy-start.9 = (f32[32,4,576]{2,0,1:T(8,128)}, f32[32,4,576]{2,0,1:T(8,128)S(1)}, u32[]{:S(2)}) copy-start(f32[32,4,576]{2,0,1:T(8,128)S(1)} %copy.73) | copy-start | bytes 884740
  4.0 15.3 %collective-permute-start = (f32[5,4,32,4]{3,2,1,0:T(8,128)}, f32[5,4,32,4]{3,2,1,0:T(8,128)}, u32[]{:S(2)}, u32[]{:S(2)}) collective-permute-start(f32[5,4,32,4]{3,2,1,0:T(8,128)} %pad_maximum_fusion.1), channel_id=1, source_target_pairs={{0,1},{1,0},{2,3},{3,2},{4,5},{5,4},{6,7},{7,6},{8,9},{9,8},{10,11... | collective-permute-start | bytes 30728 | tf_op jit(solution)/shard_map/ppermute | solution.py:261
  4.6 31.5 %collective-permute-start.3 = (f32[48,1152]{1,0:T(8,128)S(1)}, f32[48,1152]{1,0:T(8,128)S(1)}, u32[]{:S(2)}, u32[]{:S(2)}) collective-permute-start(f32[48,1152]{1,0:T(8,128)S(1)} %get-tuple-element.20), channel_id=1, source_target_pairs={{2,0},{4,2},{6,4},{8,6},{10,8},{12,10},{14,12},{3,1},{5,3},{7,5},{... | collective-permute-start | bytes 663560 | tf_op jit(solution)/shard_map/ppermute | solution.py:254
  5.9 24.3 %collective-permute-start.8 = (f32[32,1152]{1,0:T(8,128)S(1)}, f32[32,1152]{1,0:T(8,128)S(1)}, u32[]{:S(2)}, u32[]{:S(2)}) collective-permute-start(f32[32,1152]{1,0:T(8,128)S(1)} %get-tuple-element.25), channel_id=1, source_target_pairs={{0,2},{2,4},{4,6},{6,8},{8,10},{10,12},{12,14},{1,3},{3,5},{5,7},{... | collective-permute-start | bytes 442376 | tf_op jit(solution)/shard_map/ppermute | solution.py:253
  11.2 20.3 %collective-permute-start.6 = (f32[32,1152]{1,0:T(8,128)S(1)}, f32[32,1152]{1,0:T(8,128)S(1)}, u32[]{:S(2)}, u32[]{:S(2)}) collective-permute-start(f32[32,1152]{1,0:T(8,128)S(1)} %get-tuple-element.23), channel_id=1, source_target_pairs={{0,2},{2,4},{4,6},{6,8},{8,10},{10,12},{12,14},{1,3},{3,5},{5,7},{... | collective-permute-start | bytes 442376 | tf_op jit(solution)/shard_map/ppermute | solution.py:253
  16.0 21.8 %collective-permute-start.7 = (f32[32,1152]{1,0:T(8,128)S(1)}, f32[32,1152]{1,0:T(8,128)S(1)}, u32[]{:S(2)}, u32[]{:S(2)}) collective-permute-start(f32[32,1152]{1,0:T(8,128)S(1)} %get-tuple-element.24), channel_id=1, source_target_pairs={{2,0},{4,2},{6,4},{8,6},{10,8},{12,10},{14,12},{3,1},{5,3},{7,5},{... | collective-permute-start | bytes 442376 | tf_op jit(solution)/shard_map/ppermute | solution.py:254
  18.2 0.7 copy-start.15
  18.2 0.8 %copy-start.12 = (f32[4,4,576]{2,1,0:T(4,128)S(1)}, f32[4,4,576]{2,1,0:T(4,128)}, u32[]{:S(2)}) copy-start(f32[4,4,576]{2,1,0:T(4,128)} %param.18) | copy-start | bytes 110596
  18.2 0.8 %copy-start.18 = (s32[1,1,18,1]{2,3,1,0:T(1,128)S(1)}, s32[1,1,18,1]{2,3,1,0:T(1,128)}, u32[]{:S(2)}) copy-start(s32[1,1,18,1]{2,3,1,0:T(1,128)} %param.21) | copy-start | bytes 220
  19.2 19.0 %collective-permute-start.4 = (f32[32,1152]{1,0:T(8,128)}, f32[32,1152]{1,0:T(8,128)S(1)}, u32[]{:S(2)}, u32[]{:S(2)}) collective-permute-start(f32[32,1152]{1,0:T(8,128)} %get-tuple-element.21), channel_id=1, source_target_pairs={{0,2},{2,4},{4,6},{6,8},{8,10},{10,12},{12,14},{1,3},{3,5},{5,7},{... | collective-permute-start | bytes 442376 | tf_op jit(solution)/shard_map/ppermute | solution.py:253
  25.0 2.5 %copy-start.10 = (f32[32,4,576]{2,0,1:T(8,128)S(1)}, f32[32,4,576]{2,0,1:T(8,128)}, u32[]{:S(2)}) copy-start(f32[32,4,576]{2,0,1:T(8,128)} %copy-done.9) | copy-start | bytes 884740
  27.5 9.9 %copy-start.6 = (f32[32,32]{1,0:T(8,128)S(1)}, f32[32,32]{1,0:T(8,128)}, u32[]{:S(2)}) copy-start(f32[32,32]{1,0:T(8,128)} %refs_8_.1) | copy-start | bytes 12292
  30.2 8.0 %collective-permute-start.5 = (f32[32,1152]{1,0:T(8,128)}, f32[32,1152]{1,0:T(8,128)S(1)}, u32[]{:S(2)}, u32[]{:S(2)}) collective-permute-start(f32[32,1152]{1,0:T(8,128)} %get-tuple-element.22), channel_id=1, source_target_pairs={{2,0},{4,2},{6,4},{8,6},{10,8},{12,10},{14,12},{3,1},{5,3},{7,5},{... | collective-permute-start | bytes 442376 | tf_op jit(solution)/shard_map/ppermute | solution.py:254
  31.5 10.2 %collective-permute-start.1 = (f32[32,1152]{1,0:T(8,128)S(1)}, f32[32,1152]{1,0:T(8,128)S(1)}, u32[]{:S(2)}, u32[]{:S(2)}) collective-permute-start(f32[32,1152]{1,0:T(8,128)S(1)} %get-tuple-element.18), channel_id=1, source_target_pairs={{0,2},{2,4},{4,6},{6,8},{8,10},{10,12},{12,14},{1,3},{3,5},{5,7},{... | collective-permute-start | bytes 442376 | tf_op jit(solution)/shard_map/ppermute | solution.py:253
  36.0 7.5 %collective-permute-start.2 = (f32[32,1152]{1,0:T(8,128)S(1)}, f32[32,1152]{1,0:T(8,128)S(1)}, u32[]{:S(2)}, u32[]{:S(2)}) collective-permute-start(f32[32,1152]{1,0:T(8,128)S(1)} %get-tuple-element.19), channel_id=1, source_target_pairs={{2,0},{4,2},{6,4},{8,6},{10,8},{12,10},{14,12},{3,1},{5,3},{7,5},{... | collective-permute-start | bytes 442376 | tf_op jit(solution)/shard_map/ppermute | solution.py:254
  43.5 11.2 %copy-start.13 = (f32[1152]{0:T(1024)S(1)}, f32[1152]{0:T(1024)}, u32[]{:S(2)}) copy-start(f32[1152]{0:T(1024)} %constant.52.clone) | copy-start | bytes 13828
  43.5 11.2 %copy-start.14 = (f32[1152]{0:T(1024)S(1)}, f32[1152]{0:T(1024)}, u32[]{:S(2)}) copy-start(f32[1152]{0:T(1024)} %constant.54.clone) | copy-start | bytes 13828
  43.5 11.2 %copy-start.16 = (pred[1152]{0:T(1024)(128)(4,1)S(1)}, pred[1152]{0:T(1024)(128)(4,1)}, u32[]{:S(2)}) copy-start(pred[1152]{0:T(1024)(128)(4,1)} %constant.53.clone) | copy-start | bytes 3460
  43.5 13.6 %copy-start.1 = (bf16[1024,256]{1,0:T(8,128)(2,1)S(1)}, bf16[1024,256]{1,0:T(8,128)(2,1)}, u32[]{:S(2)}) copy-start(bf16[1024,256]{1,0:T(8,128)(2,1)} %constant.55.clone.refs_3_) | copy-start | bytes 1572868
  43.5 13.6 %copy-start.2 = (bf16[1024,256]{1,0:T(8,128)(2,1)S(1)}, bf16[1024,256]{1,0:T(8,128)(2,1)}, u32[]{:S(2)}) copy-start(bf16[1024,256]{1,0:T(8,128)(2,1)} %constant.56.clone.refs_4_) | copy-start | bytes 1572868
  43.5 13.6 %copy-start.4 = (bf16[128,128]{1,0:T(8,128)(2,1)S(1)}, bf16[128,128]{1,0:T(8,128)(2,1)}, u32[]{:S(2)}) copy-start(bf16[128,128]{1,0:T(8,128)(2,1)} %constant.57.clone.refs_5_) | copy-start | bytes 98308
  43.5 13.6 %copy-start.5 = (bf16[128,128]{1,0:T(8,128)(2,1)S(1)}, bf16[128,128]{1,0:T(8,128)(2,1)}, u32[]{:S(2)}) copy-start(bf16[128,128]{1,0:T(8,128)(2,1)} %constant.58.clone.refs_6_) | copy-start | bytes 98308
  43.6 13.6 %copy-start.7 = (s32[4]{0:T(128)S(1)}, s32[4]{0:T(128)}, u32[]{:S(2)}) copy-start(s32[4]{0:T(128)} %refs_0_.15) | copy-start | bytes 52
  44.1 4.4 %collective-permute-start.13 = (f32[1,128]{1,0:T(1,128)S(1)}, f32[1,128]{1,0:T(1,128)S(1)}, u32[]{:S(2)}, u32[]{:S(2)}) collective-permute-start(f32[1,128]{1,0:T(1,128)S(1)} %get-tuple-element.33), channel_id=1, source_target_pairs={{0,2},{2,0},{4,6},{6,4},{8,10},{10,8},{12,14},{14,12},{1,3},{3,1},... | collective-permute-start | bytes 1544 | tf_op jit(solution)/shard_map/ppermute | solution.py:374
  48.5 3.5 %collective-permute-start.14 = (f32[1,128]{1,0:T(1,128)S(1)}, f32[1,128]{1,0:T(1,128)S(1)}, u32[]{:S(2)}, u32[]{:S(2)}) collective-permute-start(f32[1,128]{1,0:T(1,128)S(1)} %add.48), channel_id=1, source_target_pairs={{0,4},{2,6},{4,0},{6,2},{8,12},{10,14},{12,8},{14,10},{1,5},{3,7},... | collective-permute-start | bytes 1544 | tf_op jit(solution)/shard_map/ppermute | solution.py:374
  50.2 7.0 %collective-permute-start.12 = (f32[4,32,640]{2,1,0:T(8,128)S(1)}, f32[4,32,640]{2,1,0:T(8,128)}, u32[]{:S(2)}, u32[]{:S(2)}) collective-permute-start(f32[4,32,640]{2,1,0:T(8,128)S(1)} %get-tuple-element.32.refs_1_), channel_id=1, source_target_pairs={{0,1},{1,0},{2,3},{3,2},{4,5},{5,4},{6,7},{7,6},{8,9},{9,8},{10,11... | collective-permute-start | bytes 983048 | tf_op jit(solution)/shard_map/ppermute | solution.py:339
  50.2 10.2 %collective-permute-start.11 = (f32[4,32,640]{2,1,0:T(8,128)S(1)}, f32[4,32,640]{2,1,0:T(8,128)S(1)}, u32[]{:S(2)}, u32[]{:S(2)}) collective-permute-start(f32[4,32,640]{2,1,0:T(8,128)S(1)} %get-tuple-element.31.refs_1_), channel_id=1, source_target_pairs={{0,1},{1,0},{2,3},{3,2},{4,5},{5,4},{6,7},{7,6},{8,9},{9,8},{10,11... | collective-permute-start | bytes 983048 | tf_op jit(solution)/shard_map/ppermute | solution.py:339
  50.7 12.6 %collective-permute-start.10 = (f32[4,32,640]{2,1,0:T(8,128)S(1)}, f32[4,32,640]{2,1,0:T(8,128)S(1)}, u32[]{:S(2)}, u32[]{:S(2)}) collective-permute-start(f32[4,32,640]{2,1,0:T(8,128)S(1)} %get-tuple-element.30.refs_1_), channel_id=1, source_target_pairs={{0,1},{1,0},{2,3},{3,2},{4,5},{5,4},{6,7},{7,6},{8,9},{9,8},{10,11... | collective-permute-start | bytes 983048 | tf_op jit(solution)/shard_map/ppermute | solution.py:339
  50.8 15.3 %collective-permute-start.9 = (f32[4,32,640]{2,1,0:T(8,128)S(1)}, f32[4,32,640]{2,1,0:T(8,128)S(1)}, u32[]{:S(2)}, u32[]{:S(2)}) collective-permute-start(f32[4,32,640]{2,1,0:T(8,128)S(1)} %get-tuple-element.29.refs_1_), channel_id=1, source_target_pairs={{0,1},{1,0},{2,3},{3,2},{4,5},{5,4},{6,7},{7,6},{8,9},{9,8},{10,11... | collective-permute-start | bytes 983048 | tf_op jit(solution)/shard_map/ppermute | solution.py:339
  52.1 4.4 %collective-permute-start.15 = (f32[1,128]{1,0:T(1,128)S(1)}, f32[1,128]{1,0:T(1,128)S(1)}, u32[]{:S(2)}, u32[]{:S(2)}) collective-permute-start(f32[1,128]{1,0:T(1,128)S(1)} %add.49), channel_id=1, source_target_pairs={{0,8},{2,10},{4,12},{6,14},{8,0},{10,2},{12,4},{14,6},{1,9},{3,11}... | collective-permute-start | bytes 1544 | tf_op jit(solution)/shard_map/ppermute | solution.py:374

commit v2 on v1

--- a/solution.py
+++ b/solution.py
@@ -14,7 +14,6 @@
 VMEM_BYTES = 24 * 1024 * 1024
 NEAR = 7.0 / 12.0
 FAR = 1.0 / 12.0
-DOT_LAST = (((1,), (1,)), ((), ()))
 
 
 def params():
@@ -56,7 +55,8 @@
         folded = np.minimum(whole[0], length - whole[0])
         numbers += [folded, folded]
         weights.append(np.full(2 * LANES, 2.0 / length))
-    return first, np.concatenate(others, axis=0), np.concatenate(numbers), np.concatenate(weights)
+    others += [table.T for table in others]
+    return np.concatenate([first, first.T]), np.concatenate(others), np.concatenate(numbers), np.concatenate(weights)
 
 
 def pack_rows(first, second):
@@ -74,16 +74,16 @@
     return jnp.concatenate(parts, axis=1)
 
 
-def pack_kernel(rows, levels, with_courant, *refs):
-    if with_courant:
-        tracer_ref, courant_ref, up_ref, down_ref = refs
-    else:
-        tracer_ref, up_ref, down_ref = refs
-    up_ref[...] = pack_rows(tracer_ref[0, :, rows - 2, :], tracer_ref[0, :, rows - 1, :])
-    down_ref[0:levels, :] = pack_rows(tracer_ref[0, :, 0, :], tracer_ref[0, :, 1, :])
-    if with_courant:
-        courant = courant_ref[:, 0, :]
-        down_ref[levels : levels + levels // 2, :] = pack_rows(courant[: levels // 2], courant[levels // 2 :])
+def pack_kernel(rows, levels, split, tracer_ref, courant_ref, *out_refs):
+    up_refs, down_refs = out_refs[: len(split)], out_refs[len(split) :]
+    for chunk, (begin, end) in enumerate(split):
+        for t in range(begin, end):
+            place = slice(levels * (t - begin), levels * (t - begin + 1))
+            up_refs[chunk][place, :] = pack_rows(tracer_ref[t, :, rows - 2, :], tracer_ref[t, :, rows - 1, :])
+            down_refs[chunk][place, :] = pack_rows(tracer_ref[t, :, 0, :], tracer_ref[t, :, 1, :])
+    courant = courant_ref[:, 0, :]
+    place = levels * (split[0][1] - split[0][0])
+    down_refs[0][place : place + levels // 2, :] = pack_rows(courant[: levels // 2], courant[levels // 2 :])
 
 
 def base_kernel(rows, width, padded_ref, east_courant_ref, lat_courant_ref, base_ref):
@@ -109,7 +109,8 @@
      physics_ref, energy_ref) = refs
     width = base_ref.shape[-1]
     low = low_ref[...]
-    high = high_ref[0:levels, :]
+    high = high_ref[...]
+    step = pl.program_id(0)
     low_a, low_b = low[:, :width], second_half(low, sector)
     high_a, high_b = high[:, :width], second_half(high, sector)
     courant = [courant_ref[r] for r in range(rows)]
@@ -131,10 +132,10 @@
         mixed = jnp.dot(mix, stacked, preferred_element_type=jnp.float32)
         mixed = jnp.where(level == levels - 1, mixed + surface_ref[0, r : r + 1, :], mixed)
         physics = mixed / (1.0 + decay * mixed * mixed)
-        physics_ref[r] = physics
+        physics_ref[0, r] = physics
         gap = jnp.where(lane < sector, physics - advected, 0.0)
         squared = gap * gap
-        total = energy_in_ref[r]
+        total = energy_in_ref[r] if owner_count else jnp.where(step == 0, energy_in_ref[r], energy_ref[r])
         for k in range(levels // 8):
             total = total + squared[8 * k : 8 * k + 8]
         energies.append(total)
@@ -142,22 +143,19 @@
         for r in range(rows):
             energy_ref[r] = energies[r]
         return
-    spot = lax.broadcasted_iota(jnp.int32, (1, LANES), 1)
-    result = jnp.zeros((1, LANES), jnp.float32)
     for owner in range(owner_count):
         chosen = jnp.zeros((8, LANES), jnp.float32)
         for r in range(rows):
             picked = jnp.where(owner_ref[r : r + 1, :] == owner, energies[r], 0.0)
             for k in range(width // LANES):
                 chosen = chosen + picked[:, LANES * k : LANES * (k + 1)]
-        summed = jnp.sum(jnp.sum(chosen, axis=0, keepdims=True), axis=1, keepdims=True)
-        result = jnp.where(spot == owner, summed, result)
-    energy_ref[...] = result
+        energy_ref[owner : owner + 1, :] = jnp.sum(chosen, axis=0, keepdims=True)
 
 
 def filter_kernel(rows, levels, sector, radix, has_alias, *refs):
     mask_ref, own_ref, other_ref, table_high_ref, table_low_ref, first_high_ref, first_low_ref, scale_ref = refs[:8]
     out_ref, high_ref, low_ref, wave_ref = refs[8 + has_alias :]
+    own_ref, other_ref = own_ref.at[0], other_ref.at[0]
     pairs = (radix - 1) // 2
     shift = sector % LANES
     own_segments = -(-sector // LANES)
@@ -181,26 +179,29 @@
             high_ref[levels * r : levels * (r + 1), LANES * i : LANES * (i + 1)] = part_high
             low_ref[levels * r : levels * (r + 1), LANES * i : LANES * (i + 1)] = part_low
 
-    def both_ways(begin, size, table_high, table_low):
+    def both_ways(begin, size, forward, inverse):
         count = rows * levels
 
-        def product(part_high, part_low, dims):
+        def product(part_high, part_low, table_high, table_low):
             stacked = jnp.concatenate([part_high, part_low], axis=0)
-            main = lax.dot_general(stacked, table_high, dims, preferred_element_type=jnp.float32)
-            rest = lax.dot_general(part_high, table_low, dims, preferred_element_type=jnp.float32)
+            main = jnp.dot(stacked, table_high, preferred_element_type=jnp.float32)
+            rest = jnp.dot(part_high, table_low, preferred_element_type=jnp.float32)
             return main[:count] + (main[count:] + rest)
 
-        spectrum = product(high_ref[:, begin : begin + size], low_ref[:, begin : begin + size], (((1,), (0,)), ((), ())))
+        spectrum = product(high_ref[:, begin : begin + size], low_ref[:, begin : begin + size], *forward)
         scaled = jnp.concatenate(
             [spectrum[levels * r : levels * (r + 1)] * scale_ref[r : r + 1, begin : begin + size] for r in range(rows)], axis=0
         )
-        wave_ref[:, begin : begin + size] = product(*split_high_low(scaled), DOT_LAST)
-
-    both_ways(0, LANES, first_high_ref[...], first_low_ref[...])
+        wave_ref[:, begin : begin + size] = product(*split_high_low(scaled), *inverse)
+
+    def pair_of(high, low, begin, size):
+        return high[begin : begin + size, :], low[begin : begin + size, :]
+
+    both_ways(0, LANES, *(pair_of(first_high_ref, first_low_ref, LANES * i, LANES) for i in range(2)))
     for k in range(pairs):
         both_ways(
             LANES * (2 * k + 1), 2 * LANES,
-            table_high_ref[2 * LANES * k : 2 * LANES * (k + 1), :], table_low_ref[2 * LANES * k : 2 * LANES * (k + 1), :],
+            *(pair_of(table_high_ref, table_low_ref, 2 * LANES * (k + pairs * i), 2 * LANES) for i in range(2)),
         )
 
     for r in range(rows):
@@ -235,23 +236,24 @@
     downward = [(i + 1, i) for i in range(lat_count - 1)]
     swap = [(0, 1), (1, 0)]
 
-    from_south, from_north = [], []
-    for t in range(tracer_count):
-        with_courant = t == 0
-        down_rows = levels + (levels // 2 if with_courant else 0)
-        up, down = pl.pallas_call(
-            functools.partial(pack_kernel, rows, levels, with_courant),
-            grid=(1,),
-            in_specs=[vmem((1, levels, rows, sector), (t, 0, 0, 0))]
-            + ([vmem((levels, rows, sector))] if with_courant else []),
-            out_specs=[vmem((levels, length)), vmem((down_rows, length))],
-            out_shape=[jax.ShapeDtypeStruct((levels, length), f32), jax.ShapeDtypeStruct((down_rows, length), f32)],
-            compiler_params=params(),
-            cost_estimate=cost(0, 600_000),
-            name="pack",
-        )(tracers, *([courant_lat] if with_courant else []))
-        from_south.append(lax.ppermute(up, "lat", upward))
-        from_north.append(lax.ppermute(down, "lat", downward))
+    split = [(0, tracer_count - 1), (tracer_count - 1, tracer_count)]
+    up_rows = [levels * (end - begin) for begin, end in split]
+    down_rows = [up_rows[0] + levels // 2] + up_rows[1:]
+    packed_shapes = [(count, length) for count in up_rows + down_rows]
+    packed = pl.pallas_call(
+        functools.partial(pack_kernel, rows, levels, split),
+        grid=(1,),
+        in_specs=[vmem(tracers.shape), vmem(courant_lat.shape)],
+        out_specs=[vmem(shape) for shape in packed_shapes],
+        out_shape=[jax.ShapeDtypeStruct(shape, f32) for shape in packed_shapes],
+        compiler_params=params(),
+        cost_estimate=cost(0, 600_000),
+        name="pack",
+    )(tracers, courant_lat)
+    up, down = packed[: len(split)], packed[len(split) :]
+    from_south = [lax.ppermute(up[0], "lat", upward)]
+    from_north = [lax.ppermute(down[0], "lat", downward)]
+    tracers, courant_lat, courant_lon, up, down = lax.optimization_barrier((tracers, courant_lat, courant_lon, up, down))
 
     by_row = jnp.transpose(tracers, (0, 2, 1, 3))
     lon_by_row = jnp.transpose(courant_lon, (1, 0, 2))
@@ -259,11 +261,8 @@
     ends = jnp.concatenate([by_row[..., -2:], by_row[..., :2]], axis=-1)
     lon_end = jnp.pad(lon_by_row[..., :1], ((0, 0), (0, 0), (0, 3)))
     sides = lax.ppermute(jnp.concatenate([ends, lon_end[None]], axis=0), "lon", swap)
-    gap = width - sector - 4
-    padded = jnp.concatenate(
-        [by_row, sides[:tracer_count, ..., 2:], jnp.zeros((tracer_count, rows, levels, gap), f32), sides[:tracer_count, ..., :2]],
-        axis=-1,
-    )
+    gap = jnp.zeros((tracer_count, rows, levels, width - sector - 4), f32)
+    padded = jnp.concatenate([by_row, sides[:tracer_count, ..., 2:], gap, sides[:tracer_count, ..., :2]], axis=-1)
     east_courant = jnp.concatenate(
         [lon_by_row, sides[tracer_count, ..., :1], jnp.zeros((rows, levels, width - sector - 1), f32)], axis=-1
     )
@@ -300,64 +299,62 @@
     damping = jnp.where(jnp.asarray(numbers == 0)[None], 1.0, jnp.minimum(1.0, ratio * ratio))
     scale = damping * jnp.asarray(weights, f32)[None]
 
-    top_packed = from_north[0][levels:]
+    base, scale, surface, decay, owner_of, up, down = lax.optimization_barrier((base, scale, surface, decay, owner_of, up, down))
+    from_south.append(lax.ppermute(up[1], "lat", upward))
+    from_north.append(lax.ppermute(down[1], "lat", downward))
+    top_packed = from_north[0][up_rows[0] :]
     top = jnp.concatenate([top_packed[:, :sector], top_packed[:, sector:]], axis=0)
     top = jnp.pad(top, ((0, 0), (0, width - sector)))
 
     energy = jnp.zeros((rows, 8, width), f32)
-    own_parts, other_parts = [], []
-    for t in range(tracer_count):
-        last = t == tracer_count - 1
-        energy_shape = (1, LANES) if last else (rows, 8, width)
-        down_rows = from_north[t].shape[0]
+    out = None
+    tables = (others_high, others_low, first_high, first_low)
+    for chunk, (begin, end) in enumerate(split):
+        last = chunk == len(split) - 1
+        energy_shape = (lat_count, LANES) if last else (rows, 8, width)
+        block = (1, rows, levels, width)
         physics, energy = pl.pallas_call(
             functools.partial(physics_kernel, rows, levels, sector, lat_count if last else 0),
-            grid=(1,),
+            grid=(end - begin,),
             in_specs=([vmem((rows, width))] if last else [])
             + [
-                vmem((1, rows, levels, width), (t, 0, 0, 0)),
-                vmem((1, rows, levels, width), (t, 0, 0, 0)),
-                vmem((levels, length)),
-                vmem((down_rows, length)),
+                pl.BlockSpec(block, lambda i, begin=begin: (begin + i, 0, 0, 0)),
+                pl.BlockSpec(block, lambda i, begin=begin: (begin + i, 0, 0, 0)),
+                pl.BlockSpec((levels, length), lambda i: (i, 0)),
+                pl.BlockSpec((levels, length), lambda i: (i, 0)),
                 vmem((rows, levels, width)),
                 vmem((levels, width)),
-                vmem((1, rows, width), (t, 0, 0)),
+                pl.BlockSpec((1, rows, width), lambda i, begin=begin: (begin + i, 0, 0)),
                 vmem((levels, levels)),
-                vmem((1, levels, 1), (t, 0, 0)),
+                pl.BlockSpec((1, levels, 1), lambda i, begin=begin: (begin + i, 0, 0)),
                 vmem((rows, 8, width)),
             ],
-            out_specs=[vmem((rows, levels, width)), vmem(energy_shape)],
-            out_shape=[jax.ShapeDtypeStruct((rows, levels, width), f32), jax.ShapeDtypeStruct(energy_shape, f32)],
+            out_specs=[pl.BlockSpec(block, lambda i: (i, 0, 0, 0)), vmem(energy_shape)],
+            out_shape=[jax.ShapeDtypeStruct((end - begin,) + block[1:], f32), jax.ShapeDtypeStruct(energy_shape, f32)],
             compiler_params=params(),
             cost_estimate=cost(50_000_000, 2_000_000),
             name="physics",
         )(
             *([owner_of] if last else []),
-            base, padded, from_south[t], from_north[t], lat_courant, top, surface, mixing, decay, energy,
+            base, padded, from_south[chunk], from_north[chunk], lat_courant, top, surface, mixing, decay, energy,
         )
-        own_parts.append(physics)
-        other_parts.append(lax.ppermute(physics, "lon", swap))
-
-    out = None
-    tables = (others_high, others_low, first_high, first_low)
-    for t in range(tracer_count):
+        other = lax.ppermute(physics, "lon", swap)
+        if last:
+            owner_parts = lax.all_to_all(energy, "lat", 0, 0, tiled=True)
         has_alias = int(out is not None)
         out = pl.pallas_call(
             functools.partial(filter_kernel, rows, levels, sector, radix, has_alias),
-            grid=(1,),
+            grid=(end - begin,),
             in_specs=[
                 pl.BlockSpec(memory_space=pltpu.SMEM),
-                vmem((rows, levels, width)),
-                vmem((rows, levels, width)),
-                vmem(others_high.shape),
-                vmem(others_low.shape),
-                vmem(first_high.shape),
-                vmem(first_low.shape),
-                vmem((rows, length)),
+                pl.BlockSpec(block, lambda i: (i, 0, 0, 0)),
+                pl.BlockSpec(block, lambda i: (i, 0, 0, 0)),
             ]
+            + [vmem(table.shape) for table in tables]
+            + [vmem((rows, length))]
             + [pl.BlockSpec(memory_space=pl.ANY)] * has_alias,
-            out_specs=vmem((1, levels, rows, sector), (t, 0, 0, 0)),
-            out_shape=jax.ShapeDtypeStruct(tracers.shape, f32),
+            out_specs=pl.BlockSpec((1, levels, rows, sector), lambda i, begin=begin: (begin + i, 0, 0, 0)),
+            out_shape=jax.ShapeDtypeStruct((tracer_count, levels, rows, sector), f32),
             scratch_shapes=[
                 pltpu.VMEM((rows * levels, length), jnp.bfloat16),
                 pltpu.VMEM((rows * levels, length), jnp.bfloat16),
@@ -367,13 +364,11 @@
             compiler_params=params(),
             cost_estimate=cost(450_000_000, 3_000_000),
             name="filter",
-        )(polar_mask, own_parts[t], other_parts[t], *(jnp.asarray(table) for table in tables), scale, *([out] if has_alias else []))
-
-    step = 1
-    while step < lat_count:
-        energy = energy + lax.ppermute(energy, "lat", [(i, i ^ step) for i in range(lat_count)])
-        step *= 2
-    owner_energy = lax.dynamic_slice(energy, (0, lat), (1, 1)) / (block_count * BLOCK)
+        )(polar_mask, physics, other, *(jnp.asarray(table) for table in tables), scale, *([out] if has_alias else []))
+        if not last:
+            energy, out = lax.optimization_barrier((energy, out))
+
+    owner_energy = jnp.sum(owner_parts).reshape(1, 1) / (block_count * BLOCK)
     return out, owner_energy
 
 

time: 69.6 us -> 68 us (0.977)
  starting transfers between devices: 32.9 us -> 12.8 us
  blocking collectives: 0 us -> 12.3 us
  local copies, waits for them, and re-layouts: 5.36 us -> 10.2 us
  waiting for transfers between devices: 9.09 us -> 13 us
  Pallas kernels: 17.2 us -> 14.9 us
  other arithmetic: 3.41 us -> 1.33 us
  between operations: 1.06 us -> 2.89 us
    ppermute x15 -> x6, starting transfers between devices: 32.5 us -> 12.7 us  [the longest x1 5.61 us: on_device(): from_south = [lax.ppermute(up[0], 'lat', upward)]]
    all_to_all x0 -> x1, blocking collectives: none -> 12.3 us  [on_device(): owner_parts = lax.all_to_all(energy, 'lat', 0, 0, tiled=True)]
    unnamed x40 -> x60, local copies, waits for them, and re-layouts: 2.68 us -> 7.44 us
    pallas_call x4 -> x2, Pallas kernels: 11.9 us -> 7.84 us  [on_device(): pl.pallas_call(functools.partial(filter_kernel, rows, levels, sector, rad...]
    ppermute x15 -> x6, waiting for transfers between devices: 9.08 us -> 13 us  [the longest x1 6.44 us: on_device(): from_north = [lax.ppermute(down[0], 'lat', downward)]]
    pallas_call x4 -> x2, Pallas kernels: 1.55 us -> 3.14 us  [on_device(): pl.pallas_call(functools.partial(physics_kernel, rows, levels, sector, la...]
    concatenate x1, other arithmetic: 1.62 us -> 0.25 us  [on_device(): jnp.concatenate([by_row, sides[:tracer_count, ..., 2:], gap, sides[:trace...]
    slice x1, local copies, waits for them, and re-layouts: 1.16 us -> 0.13 us  [on_device(): sides[:tracer_count, ..., 2:]]
  transfers between devices with their start and end apart: 16 -> 7, of which waited for: 5 -> 3; matrix products, arithmetic and copies ran while one was open for 7% -> 6% of each run, Pallas kernels for 20% -> 12%
where the time goes in v2:
time: 68 us; the launch traced here: 67.4 us
  Pallas kernels  14.9 us (22%)
  waiting for transfers between devices  13 us (19%)
  starting transfers between devices  12.8 us (19%)
  blocking collectives  12.3 us (18%)
  local copies, waits for them, and re-layouts  10.2 us (15%)
  between operations  2.89 us (4%)
  other arithmetic  1.33 us (2%)
    all_to_all x1, blocking collectives, on_device(): owner_parts = lax.all_to_all(energy, 'lat', 0, 0, tiled=True)  12.3 us
    pallas_call x2, Pallas kernels, on_device(): pl.pallas_call(functools.partial(filter_kernel, rows, levels, sector, rad...  7.84 us
    unnamed x60, local copies, waits for them, and re-layouts  7.44 us
    ppermute x1, waiting for transfers between devices, on_device(): from_north = [lax.ppermute(down[0], 'lat', downward)]  6.44 us
    ppermute x1, starting transfers between devices, on_device(): from_south = [lax.ppermute(up[0], 'lat', upward)]  5.61 us
    ppermute x1, waiting for transfers between devices, on_device(): from_south = [lax.ppermute(up[0], 'lat', upward)]  4.62 us
    ppermute x1, starting transfers between devices, on_device(): from_south.append(lax.ppermute(up[1], 'lat', upward))  4.39 us
    pallas_call x2, Pallas kernels, on_device(): pl.pallas_call(functools.partial(physics_kernel, rows, levels, sector, la...  3.14 us
  transfers between devices with their start and end apart: 7, of which 3 were waited for; matrix products, arithmetic and copies ran while one was open for 6% of the time, Pallas kernels for 12%

profile of v2, /device:TPU:0, one launch (start us, length us, event | category | flops | bytes accessed | tf_op | source)
XLA Modules:
  0.0 67.4 jit_solution(9086991375948690257)
XLA Ops:
  0.6 1.3 %copy-done = f32[4,32,4,576]{3,2,1,0:T(4,128)S(1)} copy-done((f32[4,32,4,576]{3,2,1,0:T(4,128)S(1)}, f32[4,32,4,576]{3,2,1,0:T(4,128)}, u32[]{:S(2)}) %copy-start) | copy-done | bytes 1179672
  1.9 1.0 %copy-done.5 = f32[32,4,576]{2,1,0:T(4,128)S(1)} copy-done((f32[32,4,576]{2,1,0:T(4,128)S(1)}, f32[32,4,576]{2,1,0:T(4,128)}, u32[]{:S(2)}) %copy-start.5) | copy-done | bytes 294936
  2.9 1.2 %pack.1 = (f32[96,1152]{1,0:T(8,128)}, f32[32,1152]{1,0:T(8,128)S(1)}, f32[112,1152]{1,0:T(8,128)}, f32[32,1152]{1,0:T(8,128)S(1)}) custom-call(f32[4,32,4,576]{3,2,1,0:T(4,128)S(1)} %copy-done, f32[32,4,576]{2,1,0:T(4,128)S(1)} %copy-done.5), custom_call_target="tpu_custom_call" | custom-call | bytes 600000 | tf_op jit(solution)/shard_map/pack/pallas_call | solution.py:243
  4.1 5.6 %collective-permute-start.4 = (f32[96,1152]{1,0:T(8,128)}, f32[96,1152]{1,0:T(8,128)}, u32[]{:S(2)}, u32[]{:S(2)}) collective-permute-start(f32[96,1152]{1,0:T(8,128)} %get-tuple-element.24), channel_id=1, source_target_pairs={{0,2},{2,4},{4,6},{6,8},{8,10},{10,12},{12,14},{1,3},{3,5},{5,7},{... | collective-permute-start | bytes 1327112 | tf_op jit(solution)/shard_map/ppermute | solution.py:254
  9.7 1.3 %collective-permute-start.3 = (f32[112,1152]{1,0:T(8,128)}, f32[112,1152]{1,0:T(8,128)S(1)}, u32[]{:S(2)}, u32[]{:S(2)}) collective-permute-start(f32[112,1152]{1,0:T(8,128)} %get-tuple-element.26), channel_id=1, source_target_pairs={{2,0},{4,2},{6,4},{8,6},{10,8},{12,10},{14,12},{3,1},{5,3},{7,5},{... | collective-permute-start | bytes 1548296 | tf_op jit(solution)/shard_map/ppermute | solution.py:255
  11.1 0.0 copy-start.19
  11.1 0.0 copy-start.28
  11.1 0.1 copy.63
  11.2 0.0 copy-done.15
  11.2 0.0 copy-done.17
  11.3 0.0 copy-start.24
  11.3 0.0 copy-start.25
  11.3 0.0 copy-start.27
  11.3 0.0 copy-start.6
  11.3 0.0 copy-start.29
  11.3 0.0 copy-start.22
  11.3 0.1 fusion.2
  11.5 0.3 copy-done.19
  11.8 0.1 pad_maximum_fusion.1
  11.9 0.1 collective-permute-start
  12.1 0.1 select_multiply_fusion.refs_7_
  12.2 0.1 copy-done.6
  12.3 0.1 fusion
  12.4 0.7 pad.32.clone
  13.1 0.1 pad.29.clone
  13.1 0.0 copy-done.29
  13.1 0.1 broadcast_in_dim.51
  13.2 0.1 reshape_reshape.3
  13.3 0.6 pad.23.refs_0_
  13.9 0.6 pad.22.refs_6_.refs_7_
  14.5 0.0 collective-permute-done
  14.6 0.1 fusion.4
  14.7 0.0 copy-done.23
  14.7 0.3 pad_maximum_fusion.padded_ref.refs_1_.refs_2_
  15.0 0.7 %copy-done.20 = f32[32,4,576]{2,0,1:T(8,128)S(1)} copy-done((f32[32,4,576]{2,0,1:T(8,128)S(1)}, f32[32,4,576]{2,0,1:T(8,128)}, u32[]{:S(2)}) %copy-start.20) | copy-done | bytes 294936
  15.7 0.1 maximum_maximum_fusion.east_courant_ref
  15.8 0.0 copy-start.26
  15.8 2.7 %base.1.refs_0_.refs_1_ = f32[4,4,32,640]{3,2,1,0:T(8,128)S(1)} custom-call(f32[4,4,32,640]{3,2,1,0:T(8,128)S(1)} %pad_maximum_fusion.padded_ref.refs_1_.refs_2_, f32[4,32,640]{2,1,0:T(8,128)S(1)} %maximum_maximum_fusion.east_courant_ref, f32[4,32,640]{2,1,0:T(8,128)S(1)} %pad.21.lat_courant_ref.refs_4_.refs_5_), custom_call_target="tpu_custom_call" | custom-call | bytes 3000000 | tf_op jit(solution)/shard_map/base/pallas_call | solution.py:271
  18.5 0.1 copy.56.refs_8_.refs_9_
  18.6 6.4 %collective-permute-done.3.refs_3_ = f32[112,1152]{1,0:T(8,128)S(1)} collective-permute-done((f32[112,1152]{1,0:T(8,128)}, f32[112,1152]{1,0:T(8,128)S(1)}, u32[]{:S(2)}, u32[]{:S(2)}) %collective-permute-start.3) | collective-permute-done | bytes 516128 | tf_op jit(solution)/shard_map/ppermute | solution.py:255
  25.0 0.1 fusion.3
  25.1 4.6 %collective-permute-done.4.refs_2_ = f32[96,1152]{1,0:T(8,128)} collective-permute-done((f32[96,1152]{1,0:T(8,128)}, f32[96,1152]{1,0:T(8,128)}, u32[]{:S(2)}, u32[]{:S(2)}) %collective-permute-start.4) | collective-permute-done | bytes 442400 | tf_op jit(solution)/shard_map/ppermute | solution.py:254
  29.8 0.8 %copy-done.7 = f32[4,4,640]{2,1,0:T(4,128)S(1)} copy-done((f32[4,4,640]{2,1,0:T(4,128)S(1)}, f32[4,4,640]{2,1,0:T(4,128)}, u32[]{:S(2)}) %copy-start.7) | copy-done | bytes 40984
  30.5 0.7 %copy-done.12 = f32[32,32]{1,0:T(8,128)S(1)} copy-done((f32[32,32]{1,0:T(8,128)S(1)}, f32[32,32]{1,0:T(8,128)}, u32[]{:S(2)}) %copy-start.12) | copy-done | bytes 4120
  31.3 0.0 copy-start.8
  31.3 0.0 copy-start.10
  31.3 0.0 copy-start.14
  31.3 2.7 %physics.2 = (f32[3,4,32,640]{3,2,1,0:T(8,128)S(1)}, f32[4,8,640]{2,1,0:T(8,128)S(1)}) custom-call(f32[4,4,32,640]{3,2,1,0:T(8,128)S(1)} %base.1.refs_0_.refs_1_, f32[4,4,32,640]{3,2,1,0:T(8,128)S(1)} %pad_maximum_fusion.padded_ref.refs_1_.refs_2_, f32[96,1152]{1,0:T(8,128)} %collective-permute-done.4.refs_2_, ...), custom_call_target="tpu_custom_call" | custom-call | flops 50000000 | bytes 2000000 | tf_op jit(solution)/shard_map/physics/pallas_call | solution.py:316
  34.0 0.1 collective-permute-start.5
  34.1 4.4 %collective-permute-start.1 = (f32[32,1152]{1,0:T(8,128)S(1)}, f32[32,1152]{1,0:T(8,128)S(1)}, u32[]{:S(2)}, u32[]{:S(2)}) collective-permute-start(f32[32,1152]{1,0:T(8,128)S(1)} %copy-done.18), channel_id=1, source_target_pairs={{0,2},{2,4},{4,6},{6,8},{8,10},{10,12},{12,14},{1,3},{3,5},{5,7},{... | collective-permute-start | bytes 442376 | tf_op jit(solution)/shard_map/ppermute | solution.py:303
  38.5 1.3 %collective-permute-start.2 = (f32[32,1152]{1,0:T(8,128)S(1)}, f32[32,1152]{1,0:T(8,128)S(1)}, u32[]{:S(2)}, u32[]{:S(2)}) collective-permute-start(f32[32,1152]{1,0:T(8,128)S(1)} %copy-done.16), channel_id=1, source_target_pairs={{2,0},{4,2},{6,4},{8,6},{10,8},{12,10},{14,12},{3,1},{5,3},{7,5},{... | collective-permute-start | bytes 442376 | tf_op jit(solution)/shard_map/ppermute | solution.py:304
  39.8 0.0 collective-permute-done.5.refs_2_
  39.9 5.3 %filter.2.refs_8_ = f32[4,32,4,576]{3,2,1,0:T(4,128)} custom-call(s32[4]{0:T(128)S(1)} %copy-done.14, f32[3,4,32,640]{3,2,1,0:T(8,128)S(1)} %get-tuple-element.40.refs_1_, f32[3,4,32,640]{3,2,1,0:T(8,128)S(1)} %collective-permute-done.5.refs_2_, bf16[2048,256]{1,0:T(8,128)(2,1)S(1)} %copy-done.3, bf16[2048,256]{1,0:T(8,128)(2,1)S(1)} %copy-done.1, ...), custom_call_target="tpu_custom_call" | custom-call | flops 450000000 | bytes 3000000 | tf_op jit(solution)/shard_map/filter/pallas_call | solution.py:345
  45.2 0.0 collective-permute-done.1.refs_3_
  45.2 1.9 %collective-permute-done.2.refs_4_ = f32[32,1152]{1,0:T(8,128)S(1)} collective-permute-done((f32[32,1152]{1,0:T(8,128)S(1)}, f32[32,1152]{1,0:T(8,128)S(1)}, u32[]{:S(2)}, u32[]{:S(2)}) %collective-permute-start.2) | collective-permute-done | bytes 147488 | tf_op jit(solution)/shard_map/ppermute | solution.py:304
  47.1 0.4 physics.3
  47.5 0.1 collective-permute-start.6
  47.6 12.3 %all_to_all.9 = f32[8,1,128]{2,1,0:T(1,128)S(1)} all-to-all(f32[8,1,128]{2,1,0:T(1,128)S(1)} %bitcast.18), channel_id=1, replica_groups=mesh['group'=2,'lat'=8,'lon'=2] {'lat'}, dimensions={0} | all-to-all | bytes 8192 | tf_op jit(solution)/shard_map/all_to_all | solution.py:343
  59.9 0.6 reduce_sum.9
  61.2 0.0 collective-permute-done.6.refs_2_
  61.2 0.0 copy-start.2
  61.2 1.2 %copy-done.2 = bf16[2048,256]{1,0:T(8,128)(2,1)S(1)} copy-done((bf16[2048,256]{1,0:T(8,128)(2,1)S(1)}, bf16[2048,256]{1,0:T(8,128)(2,1)}, u32[]{:S(2)}) %copy-start.2) | copy-done | bytes 1048600
  62.4 1.2 %copy-done.4 = bf16[2048,256]{1,0:T(8,128)(2,1)S(1)} copy-done((bf16[2048,256]{1,0:T(8,128)(2,1)S(1)}, bf16[2048,256]{1,0:T(8,128)(2,1)}, u32[]{:S(2)}) %copy-start.4) | copy-done | bytes 1048600
  63.7 2.6 %filter.3 = f32[4,32,4,576]{3,2,1,0:T(4,128)} custom-call(s32[4]{0:T(128)S(1)} %copy-done.14, f32[1,4,32,640]{3,2,1,0:T(8,128)S(1)} %get-tuple-element.43.refs_1_, f32[1,4,32,640]{3,2,1,0:T(8,128)S(1)} %collective-permute-done.6.refs_2_, bf16[2048,256]{1,0:T(8,128)(2,1)S(1)} %copy-done.4, ...), custom_call_target="tpu_custom_call", output_to_operand_aliasing={{}: (8, {})} | custom-call | flops 450000000 | bytes 3000000 | tf_op jit(solution)/shard_map/filter/pallas_call | solution.py:345
  (44 shorter events, 0.2 us)
Async XLA Ops:
  0.6 1.3 %copy-start = (f32[4,32,4,576]{3,2,1,0:T(4,128)S(1)}, f32[4,32,4,576]{3,2,1,0:T(4,128)}, u32[]{:S(2)}) copy-start(f32[4,32,4,576]{3,2,1,0:T(4,128)} %tracer_ref.1) | copy-start | bytes 3538948
  1.9 1.0 %copy-start.5 = (f32[32,4,576]{2,1,0:T(4,128)S(1)}, f32[32,4,576]{2,1,0:T(4,128)}, u32[]{:S(2)}) copy-start(f32[32,4,576]{2,1,0:T(4,128)} %courant_ref.1) | copy-start | bytes 884740
  2.9 8.1 %copy-start.21 = (f32[32,4,576]{2,1,0:T(4,128)S(1)}, f32[32,4,576]{2,1,0:T(4,128)}, u32[]{:S(2)}) copy-start(f32[32,4,576]{2,1,0:T(4,128)} %param.17) | copy-start | bytes 884740
  4.1 7.1 %copy-start.15 = (f32[32,1152]{1,0:T(8,128)}, f32[32,1152]{1,0:T(8,128)S(1)}, u32[]{:S(2)}) copy-start(f32[32,1152]{1,0:T(8,128)S(1)} %get-tuple-element.36) | copy-start | bytes 442372
  4.1 7.1 %copy-start.17 = (f32[32,1152]{1,0:T(8,128)}, f32[32,1152]{1,0:T(8,128)S(1)}, u32[]{:S(2)}) copy-start(f32[32,1152]{1,0:T(8,128)S(1)} %get-tuple-element.35) | copy-start | bytes 442372
  4.1 25.6 %collective-permute-start.4 = (f32[96,1152]{1,0:T(8,128)}, f32[96,1152]{1,0:T(8,128)}, u32[]{:S(2)}, u32[]{:S(2)}) collective-permute-start(f32[96,1152]{1,0:T(8,128)} %get-tuple-element.24), channel_id=1, source_target_pairs={{0,2},{2,4},{4,6},{6,8},{8,10},{10,12},{12,14},{1,3},{3,5},{5,7},{... | collective-permute-start | bytes 1327112 | tf_op jit(solution)/shard_map/ppermute | solution.py:254
  9.7 15.3 %collective-permute-start.3 = (f32[112,1152]{1,0:T(8,128)}, f32[112,1152]{1,0:T(8,128)S(1)}, u32[]{:S(2)}, u32[]{:S(2)}) collective-permute-start(f32[112,1152]{1,0:T(8,128)} %get-tuple-element.26), channel_id=1, source_target_pairs={{2,0},{4,2},{6,4},{8,6},{10,8},{12,10},{14,12},{3,1},{5,3},{7,5},{... | collective-permute-start | bytes 1548296 | tf_op jit(solution)/shard_map/ppermute | solution.py:255
  11.1 0.7 %copy-start.19 = (f32[32,4,576]{2,0,1:T(8,128)}, f32[32,4,576]{2,0,1:T(8,128)S(1)}, u32[]{:S(2)}) copy-start(f32[32,4,576]{2,0,1:T(8,128)S(1)} %copy.64) | copy-start | bytes 884740
  11.1 0.7 %copy-start.28 = (pred[4]{0:T(512)(128)(4,1)S(1)}, pred[4]{0:T(512)(128)(4,1)}, u32[]{:S(2)}) copy-start(pred[4]{0:T(512)(128)(4,1)} %constant.20.clone.1) | copy-start | bytes 16
  11.3 0.8 %copy-start.24 = (f32[1152]{0:T(1024)S(1)}, f32[1152]{0:T(1024)}, u32[]{:S(2)}) copy-start(f32[1152]{0:T(1024)} %constant.53.clone) | copy-start | bytes 13828
  11.3 0.8 %copy-start.25 = (f32[1152]{0:T(1024)S(1)}, f32[1152]{0:T(1024)}, u32[]{:S(2)}) copy-start(f32[1152]{0:T(1024)} %constant.51.clone) | copy-start | bytes 13828
  11.3 0.8 %copy-start.27 = (pred[1152]{0:T(1024)(128)(4,1)S(1)}, pred[1152]{0:T(1024)(128)(4,1)}, u32[]{:S(2)}) copy-start(pred[1152]{0:T(1024)(128)(4,1)} %constant.52.clone) | copy-start | bytes 3460
  11.3 1.0 %copy-start.6 = (f32[32,4,576]{2,1,0:T(4,128)S(1)}, f32[32,4,576]{2,1,0:T(4,128)}, u32[]{:S(2)}) copy-start(f32[32,4,576]{2,1,0:T(4,128)} %courant_ref.1) | copy-start | bytes 884740
  11.3 1.8 %copy-start.29 = (s32[1,1,18,1]{2,3,1,0:T(1,128)S(1)}, s32[1,1,18,1]{2,3,1,0:T(1,128)}, u32[]{:S(2)}) copy-start(s32[1,1,18,1]{2,3,1,0:T(1,128)} %param.21) | copy-start | bytes 220
  11.3 2.6 %copy-start.22 = (f32[4,4,576]{2,1,0:T(4,128)S(1)}, f32[4,4,576]{2,1,0:T(4,128)}, u32[]{:S(2)}) copy-start(f32[4,4,576]{2,1,0:T(4,128)} %param.18) | copy-start | bytes 110596
  11.9 2.6 %collective-permute-start = (f32[5,4,32,4]{3,2,1,0:T(8,128)S(1)}, f32[5,4,32,4]{3,2,1,0:T(8,128)S(1)}, u32[]{:S(2)}, u32[]{:S(2)}) collective-permute-start(f32[5,4,32,4]{3,2,1,0:T(8,128)S(1)} %pad_maximum_fusion.1), channel_id=1, source_target_pairs={{0,1},{1,0},{2,3},{3,2},{4,5},{5,4},{6,7},{7,6},{8,9},{9,8},{10,11... | collective-permute-start | bytes 30728 | tf_op jit(solution)/shard_map/ppermute | solution.py:263
  13.3 1.4 %copy-start.23 = (f32[640]{0:T(1024)S(1)}, f32[640]{0:T(1024)}, u32[]{:S(2)}) copy-start(f32[640]{0:T(1024)} %pad.32.clone) | copy-start | bytes 7684
  14.7 1.0 %copy-start.20 = (f32[32,4,576]{2,0,1:T(8,128)S(1)}, f32[32,4,576]{2,0,1:T(8,128)}, u32[]{:S(2)}) copy-start(f32[32,4,576]{2,0,1:T(8,128)} %copy-done.19) | copy-start | bytes 884740
  15.8 2.7 %copy-start.26 = (f32[4,32]{1,0:T(4,128)S(1)}, f32[4,32]{1,0:T(4,128)}, u32[]{:S(2)}) copy-start(f32[4,32]{1,0:T(4,128)} %param.20) | copy-start | bytes 1540
  29.8 0.8 %copy-start.7 = (f32[4,4,640]{2,1,0:T(4,128)S(1)}, f32[4,4,640]{2,1,0:T(4,128)}, u32[]{:S(2)}) copy-start(f32[4,4,640]{2,1,0:T(4,128)} %pad.22.refs_6_.refs_7_) | copy-start | bytes 122884
  30.5 0.7 %copy-start.12 = (f32[32,32]{1,0:T(8,128)S(1)}, f32[32,32]{1,0:T(8,128)}, u32[]{:S(2)}) copy-start(f32[32,32]{1,0:T(8,128)} %refs_8_.1) | copy-start | bytes 12292
  31.3 2.9 %copy-start.18 = (f32[32,1152]{1,0:T(8,128)S(1)}, f32[32,1152]{1,0:T(8,128)}, u32[]{:S(2)}) copy-start(f32[32,1152]{1,0:T(8,128)} %copy-done.17) | copy-start | bytes 442372
  31.3 7.3 %copy-start.16 = (f32[32,1152]{1,0:T(8,128)S(1)}, f32[32,1152]{1,0:T(8,128)}, u32[]{:S(2)}) copy-start(f32[32,1152]{1,0:T(8,128)} %copy-done.15) | copy-start | bytes 442372
  31.3 8.6 %copy-start.1 = (bf16[2048,256]{1,0:T(8,128)(2,1)S(1)}, bf16[2048,256]{1,0:T(8,128)(2,1)}, u32[]{:S(2)}) copy-start(bf16[2048,256]{1,0:T(8,128)(2,1)} %constant.55.clone.refs_4_) | copy-start | bytes 3145732
  31.3 8.6 %copy-start.3 = (bf16[2048,256]{1,0:T(8,128)(2,1)S(1)}, bf16[2048,256]{1,0:T(8,128)(2,1)}, u32[]{:S(2)}) copy-start(bf16[2048,256]{1,0:T(8,128)(2,1)} %constant.54.clone.refs_3_) | copy-start | bytes 3145732
  31.3 8.6 %copy-start.8 = (bf16[256,128]{1,0:T(8,128)(2,1)S(1)}, bf16[256,128]{1,0:T(8,128)(2,1)}, u32[]{:S(2)}) copy-start(bf16[256,128]{1,0:T(8,128)(2,1)} %constant.57.clone.refs_6_) | copy-start | bytes 196612
  31.3 8.6 %copy-start.10 = (bf16[256,128]{1,0:T(8,128)(2,1)S(1)}, bf16[256,128]{1,0:T(8,128)(2,1)}, u32[]{:S(2)}) copy-start(bf16[256,128]{1,0:T(8,128)(2,1)} %constant.56.clone.refs_5_) | copy-start | bytes 196612
  31.3 8.6 %copy-start.14 = (s32[4]{0:T(128)S(1)}, s32[4]{0:T(128)}, u32[]{:S(2)}) copy-start(s32[4]{0:T(128)} %refs_0_.3) | copy-start | bytes 52
  34.0 13.1 %copy-start.13 = (s32[4,640]{1,0:T(4,128)S(1)}, s32[4,640]{1,0:T(4,128)}, u32[]{:S(2)}) copy-start(s32[4,640]{1,0:T(4,128)} %pad.23.refs_0_) | copy-start | bytes 30724
  34.0 5.8 %collective-permute-start.5 = (f32[3,4,32,640]{3,2,1,0:T(8,128)S(1)}, f32[3,4,32,640]{3,2,1,0:T(8,128)S(1)}, u32[]{:S(2)}, u32[]{:S(2)}) collective-permute-start(f32[3,4,32,640]{3,2,1,0:T(8,128)S(1)} %get-tuple-element.40.refs_1_), channel_id=1, source_target_pairs={{0,1},{1,0},{2,3},{3,2},{4,5},{5,4},{6,7},{7,6},{8,9},{9,8},{10,11... | collective-permute-start | bytes 2949128 | tf_op jit(solution)/shard_map/ppermute | solution.py:341
  34.1 11.1 %collective-permute-start.1 = (f32[32,1152]{1,0:T(8,128)S(1)}, f32[32,1152]{1,0:T(8,128)S(1)}, u32[]{:S(2)}, u32[]{:S(2)}) collective-permute-start(f32[32,1152]{1,0:T(8,128)S(1)} %copy-done.18), channel_id=1, source_target_pairs={{0,2},{2,4},{4,6},{6,8},{8,10},{10,12},{12,14},{1,3},{3,5},{5,7},{... | collective-permute-start | bytes 442376 | tf_op jit(solution)/shard_map/ppermute | solution.py:303
  38.5 8.6 %collective-permute-start.2 = (f32[32,1152]{1,0:T(8,128)S(1)}, f32[32,1152]{1,0:T(8,128)S(1)}, u32[]{:S(2)}, u32[]{:S(2)}) collective-permute-start(f32[32,1152]{1,0:T(8,128)S(1)} %copy-done.16), channel_id=1, source_target_pairs={{2,0},{4,2},{6,4},{8,6},{10,8},{12,10},{14,12},{3,1},{5,3},{7,5},{... | collective-permute-start | bytes 442376 | tf_op jit(solution)/shard_map/ppermute | solution.py:304
  45.2 16.0 %copy-start.9 = (bf16[256,128]{1,0:T(8,128)(2,1)S(1)}, bf16[256,128]{1,0:T(8,128)(2,1)}, u32[]{:S(2)}) copy-start(bf16[256,128]{1,0:T(8,128)(2,1)} %constant.57.clone.refs_6_) | copy-start | bytes 196612
  45.2 16.0 %copy-start.11 = (bf16[256,128]{1,0:T(8,128)(2,1)S(1)}, bf16[256,128]{1,0:T(8,128)(2,1)}, u32[]{:S(2)}) copy-start(bf16[256,128]{1,0:T(8,128)(2,1)} %constant.56.clone.refs_5_) | copy-start | bytes 196612
  47.5 13.6 %collective-permute-start.6 = (f32[1,4,32,640]{3,2,1,0:T(8,128)S(1)}, f32[1,4,32,640]{3,2,1,0:T(8,128)S(1)}, u32[]{:S(2)}, u32[]{:S(2)}) collective-permute-start(f32[1,4,32,640]{3,2,1,0:T(8,128)S(1)} %get-tuple-element.43.refs_1_), channel_id=1, source_target_pairs={{0,1},{1,0},{2,3},{3,2},{4,5},{5,4},{6,7},{7,6},{8,9},{9,8},{10,11... | collective-permute-start | bytes 983048 | tf_op jit(solution)/shard_map/ppermute | solution.py:341
  61.2 1.2 %copy-start.2 = (bf16[2048,256]{1,0:T(8,128)(2,1)S(1)}, bf16[2048,256]{1,0:T(8,128)(2,1)}, u32[]{:S(2)}) copy-start(bf16[2048,256]{1,0:T(8,128)(2,1)} %constant.55.clone.refs_4_) | copy-start | bytes 3145732
  62.4 1.2 %copy-start.4 = (bf16[2048,256]{1,0:T(8,128)(2,1)S(1)}, bf16[2048,256]{1,0:T(8,128)(2,1)}, u32[]{:S(2)}) copy-start(bf16[2048,256]{1,0:T(8,128)(2,1)} %constant.54.clone.refs_3_) | copy-start | bytes 3145732

commit v3 on v2

--- a/solution.py
+++ b/solution.py
@@ -11,7 +11,7 @@
 
 LANES = 128
 BLOCK = 128
-VMEM_BYTES = 24 * 1024 * 1024
+VMEM_BYTES = 12 * 1024 * 1024
 NEAR = 7.0 / 12.0
 FAR = 1.0 / 12.0
 
@@ -74,16 +74,19 @@
     return jnp.concatenate(parts, axis=1)
 
 
-def pack_kernel(rows, levels, split, tracer_ref, courant_ref, *out_refs):
-    up_refs, down_refs = out_refs[: len(split)], out_refs[len(split) :]
-    for chunk, (begin, end) in enumerate(split):
-        for t in range(begin, end):
-            place = slice(levels * (t - begin), levels * (t - begin + 1))
-            up_refs[chunk][place, :] = pack_rows(tracer_ref[t, :, rows - 2, :], tracer_ref[t, :, rows - 1, :])
-            down_refs[chunk][place, :] = pack_rows(tracer_ref[t, :, 0, :], tracer_ref[t, :, 1, :])
+def pack_kernel(tracer_count, rows, levels, tracer_hbm, courant_hbm, up_ref, down_ref, tracer_ref, courant_ref, sems):
+    copies = [pltpu.make_async_copy(tracer_hbm.at[t], tracer_ref.at[t], sems.at[t]) for t in range(tracer_count)]
+    copies.append(pltpu.make_async_copy(courant_hbm, courant_ref, sems.at[tracer_count]))
+    for copy in copies:
+        copy.start()
+    for t in range(tracer_count):
+        copies[t].wait()
+        place = slice(levels * t, levels * (t + 1))
+        up_ref[place, :] = pack_rows(tracer_ref[t, :, rows - 2, :], tracer_ref[t, :, rows - 1, :])
+        down_ref[place, :] = pack_rows(tracer_ref[t, :, 0, :], tracer_ref[t, :, 1, :])
+    copies[tracer_count].wait()
     courant = courant_ref[:, 0, :]
-    place = levels * (split[0][1] - split[0][0])
-    down_refs[0][place : place + levels // 2, :] = pack_rows(courant[: levels // 2], courant[levels // 2 :])
+    down_ref[levels * tracer_count :, :] = pack_rows(courant[: levels // 2], courant[levels // 2 :])
 
 
 def base_kernel(rows, width, padded_ref, east_courant_ref, lat_courant_ref, base_ref):
@@ -102,47 +105,45 @@
         base_ref[0, r] = value
 
 
-def physics_kernel(rows, levels, sector, owner_count, *refs):
-    if owner_count:
-        owner_ref, refs = refs[0], refs[1:]
-    (base_ref, padded_ref, low_ref, high_ref, courant_ref, top_ref, surface_ref, mixing_ref, decay_ref, energy_in_ref,
-     physics_ref, energy_ref) = refs
+def physics_kernel(groups, rows, levels, sector, owner_count, *refs):
+    (owner_ref, base_ref, padded_ref, low_ref, high_ref, courant_ref, surface_ref, mixing_ref, decay_ref) = refs[:9]
+    physics_refs, energy_ref = refs[9:-1], refs[-1]
     width = base_ref.shape[-1]
-    low = low_ref[...]
-    high = high_ref[...]
-    step = pl.program_id(0)
-    low_a, low_b = low[:, :width], second_half(low, sector)
-    high_a, high_b = high[:, :width], second_half(high, sector)
+    tracer_count = base_ref.shape[0]
     courant = [courant_ref[r] for r in range(rows)]
-    south = courant[0] * (NEAR * low_b - FAR * low_a)
-    south_in = courant[1] * (FAR * low_b)
-    north_in = courant[3] * (FAR * high_a)
-    north = top_ref[...] * (NEAR * (high_a + padded_ref[0, 3]) - FAR * (high_b + padded_ref[0, 2]))
-    extra = [south + south_in, -south_in, north_in, -north_in - north]
+    top = high_ref[levels * tracer_count :, :]
+    top = jnp.concatenate([top[:, :width], second_half(top, sector)], axis=0)
     mix_high, mix_low = split_high_low(mixing_ref[...])
     mix = jnp.concatenate([mix_high, mix_high, mix_low, mix_low], axis=1)
-    decay = decay_ref[0]
     level = lax.broadcasted_iota(jnp.int32, (levels, width), 0)
     lane = lax.broadcasted_iota(jnp.int32, (levels, width), 1)
-    energies = []
-    for r in range(rows):
-        advected = base_ref[0, r] + extra[r]
-        part_high, part_low = split_high_low(advected)
-        stacked = jnp.concatenate([part_high, part_low, part_high, part_low], axis=0)
-        mixed = jnp.dot(mix, stacked, preferred_element_type=jnp.float32)
-        mixed = jnp.where(level == levels - 1, mixed + surface_ref[0, r : r + 1, :], mixed)
-        physics = mixed / (1.0 + decay * mixed * mixed)
-        physics_ref[0, r] = physics
-        gap = jnp.where(lane < sector, physics - advected, 0.0)
-        squared = gap * gap
-        total = energy_in_ref[r] if owner_count else jnp.where(step == 0, energy_in_ref[r], energy_ref[r])
-        for k in range(levels // 8):
-            total = total + squared[8 * k : 8 * k + 8]
-        energies.append(total)
-    if not owner_count:
-        for r in range(rows):
-            energy_ref[r] = energies[r]
-        return
+    energies = [None] * rows
+    for physics_ref, (begin, end) in zip(physics_refs, groups):
+        for t in range(begin, end):
+            low = low_ref[levels * t : levels * (t + 1), :]
+            high = high_ref[levels * t : levels * (t + 1), :]
+            low_a, low_b = low[:, :width], second_half(low, sector)
+            high_a, high_b = high[:, :width], second_half(high, sector)
+            south = courant[0] * (NEAR * low_b - FAR * low_a)
+            south_in = courant[1] * (FAR * low_b)
+            north_in = courant[3] * (FAR * high_a)
+            north = top * (NEAR * (high_a + padded_ref[t, 3]) - FAR * (high_b + padded_ref[t, 2]))
+            extra = [south + south_in, -south_in, north_in, -north_in - north]
+            for r in range(rows):
+                advected = base_ref[t, r] + extra[r]
+                part_high, part_low = split_high_low(advected)
+                stacked = jnp.concatenate([part_high, part_low, part_high, part_low], axis=0)
+                mixed = jnp.dot(mix, stacked, preferred_element_type=jnp.float32)
+                mixed = jnp.where(level == levels - 1, mixed + surface_ref[t, r : r + 1, :], mixed)
+                physics = mixed / (1.0 + decay_ref[t] * mixed * mixed)
+                physics_ref[t - begin, r] = physics
+                gap = physics - advected
+                squared = gap * gap
+                total = squared[0:8]
+                for k in range(1, levels // 8):
+                    total = total + squared[8 * k : 8 * k + 8]
+                energies[r] = total if energies[r] is None else energies[r] + total
+    energies = [jnp.where(lane[0:8] < sector, energy, 0.0) for energy in energies]
     for owner in range(owner_count):
         chosen = jnp.zeros((8, LANES), jnp.float32)
         for r in range(rows):
@@ -155,7 +156,8 @@
 def filter_kernel(rows, levels, sector, radix, has_alias, *refs):
     mask_ref, own_ref, other_ref, table_high_ref, table_low_ref, first_high_ref, first_low_ref, scale_ref = refs[:8]
     out_ref, high_ref, low_ref, wave_ref = refs[8 + has_alias :]
-    own_ref, other_ref = own_ref.at[0], other_ref.at[0]
+    step = pl.program_id(0)
+    own_ref, other_ref = own_ref.at[step], other_ref.at[step]
     pairs = (radix - 1) // 2
     shift = sector % LANES
     own_segments = -(-sector // LANES)
@@ -236,23 +238,26 @@
     downward = [(i + 1, i) for i in range(lat_count - 1)]
     swap = [(0, 1), (1, 0)]
 
-    split = [(0, tracer_count - 1), (tracer_count - 1, tracer_count)]
-    up_rows = [levels * (end - begin) for begin, end in split]
-    down_rows = [up_rows[0] + levels // 2] + up_rows[1:]
-    packed_shapes = [(count, length) for count in up_rows + down_rows]
-    packed = pl.pallas_call(
-        functools.partial(pack_kernel, rows, levels, split),
-        grid=(1,),
-        in_specs=[vmem(tracers.shape), vmem(courant_lat.shape)],
-        out_specs=[vmem(shape) for shape in packed_shapes],
-        out_shape=[jax.ShapeDtypeStruct(shape, f32) for shape in packed_shapes],
+    whole = pl.BlockSpec(memory_space=pltpu.VMEM)
+    in_hbm = pl.BlockSpec(memory_space=pltpu.HBM)
+    up_shape = (levels * tracer_count, length)
+    down_shape = (levels * tracer_count + levels // 2, length)
+    up, down = pl.pallas_call(
+        functools.partial(pack_kernel, tracer_count, rows, levels),
+        in_specs=[in_hbm, in_hbm],
+        out_specs=[whole, whole],
+        out_shape=[jax.ShapeDtypeStruct(up_shape, f32), jax.ShapeDtypeStruct(down_shape, f32)],
+        scratch_shapes=[
+            pltpu.VMEM(tracers.shape, f32),
+            pltpu.VMEM(courant_lat.shape, f32),
+            pltpu.SemaphoreType.DMA((tracer_count + 1,)),
+        ],
         compiler_params=params(),
         cost_estimate=cost(0, 600_000),
         name="pack",
     )(tracers, courant_lat)
-    up, down = packed[: len(split)], packed[len(split) :]
-    from_south = [lax.ppermute(up[0], "lat", upward)]
-    from_north = [lax.ppermute(down[0], "lat", downward)]
+    from_south = lax.ppermute(up, "lat", upward)
+    from_north = lax.ppermute(down, "lat", downward)
     tracers, courant_lat, courant_lon, up, down = lax.optimization_barrier((tracers, courant_lat, courant_lon, up, down))
 
     by_row = jnp.transpose(tracers, (0, 2, 1, 3))
@@ -299,76 +304,56 @@
     damping = jnp.where(jnp.asarray(numbers == 0)[None], 1.0, jnp.minimum(1.0, ratio * ratio))
     scale = damping * jnp.asarray(weights, f32)[None]
 
-    base, scale, surface, decay, owner_of, up, down = lax.optimization_barrier((base, scale, surface, decay, owner_of, up, down))
-    from_south.append(lax.ppermute(up[1], "lat", upward))
-    from_north.append(lax.ppermute(down[1], "lat", downward))
-    top_packed = from_north[0][up_rows[0] :]
-    top = jnp.concatenate([top_packed[:, :sector], top_packed[:, sector:]], axis=0)
-    top = jnp.pad(top, ((0, 0), (0, width - sector)))
-
-    energy = jnp.zeros((rows, 8, width), f32)
+    groups = [(0, 1), (1, 2), (2, tracer_count)]
+    physics_shapes = [(end - begin, rows, levels, width) for begin, end in groups]
+    *physics, energy = pl.pallas_call(
+        functools.partial(physics_kernel, groups, rows, levels, sector, lat_count),
+        in_specs=[whole] * 9,
+        out_specs=[whole] * (len(groups) + 1),
+        out_shape=[jax.ShapeDtypeStruct(shape, f32) for shape in physics_shapes + [(lat_count, LANES)]],
+        compiler_params=params(),
+        cost_estimate=cost(50_000_000, 4_000_000),
+        name="physics",
+    )(owner_of, base, padded, from_south, from_north, lat_courant, surface, mixing, decay)
+    other = [lax.ppermute(part, "lon", swap) for part in physics]
+
     out = None
-    tables = (others_high, others_low, first_high, first_low)
-    for chunk, (begin, end) in enumerate(split):
-        last = chunk == len(split) - 1
-        energy_shape = (lat_count, LANES) if last else (rows, 8, width)
-        block = (1, rows, levels, width)
-        physics, energy = pl.pallas_call(
-            functools.partial(physics_kernel, rows, levels, sector, lat_count if last else 0),
-            grid=(end - begin,),
-            in_specs=([vmem((rows, width))] if last else [])
-            + [
-                pl.BlockSpec(block, lambda i, begin=begin: (begin + i, 0, 0, 0)),
-                pl.BlockSpec(block, lambda i, begin=begin: (begin + i, 0, 0, 0)),
-                pl.BlockSpec((levels, length), lambda i: (i, 0)),
-                pl.BlockSpec((levels, length), lambda i: (i, 0)),
-                vmem((rows, levels, width)),
-                vmem((levels, width)),
-                pl.BlockSpec((1, rows, width), lambda i, begin=begin: (begin + i, 0, 0)),
-                vmem((levels, levels)),
-                pl.BlockSpec((1, levels, 1), lambda i, begin=begin: (begin + i, 0, 0)),
-                vmem((rows, 8, width)),
-            ],
-            out_specs=[pl.BlockSpec(block, lambda i: (i, 0, 0, 0)), vmem(energy_shape)],
-            out_shape=[jax.ShapeDtypeStruct((end - begin,) + block[1:], f32), jax.ShapeDtypeStruct(energy_shape, f32)],
-            compiler_params=params(),
-            cost_estimate=cost(50_000_000, 2_000_000),
-            name="physics",
-        )(
-            *([owner_of] if last else []),
-            base, padded, from_south[chunk], from_north[chunk], lat_courant, top, surface, mixing, decay, energy,
-        )
-        other = lax.ppermute(physics, "lon", swap)
-        if last:
-            owner_parts = lax.all_to_all(energy, "lat", 0, 0, tiled=True)
-        has_alias = int(out is not None)
-        out = pl.pallas_call(
-            functools.partial(filter_kernel, rows, levels, sector, radix, has_alias),
-            grid=(end - begin,),
-            in_specs=[
-                pl.BlockSpec(memory_space=pltpu.SMEM),
-                pl.BlockSpec(block, lambda i: (i, 0, 0, 0)),
-                pl.BlockSpec(block, lambda i: (i, 0, 0, 0)),
-            ]
-            + [vmem(table.shape) for table in tables]
-            + [vmem((rows, length))]
-            + [pl.BlockSpec(memory_space=pl.ANY)] * has_alias,
-            out_specs=pl.BlockSpec((1, levels, rows, sector), lambda i, begin=begin: (begin + i, 0, 0, 0)),
-            out_shape=jax.ShapeDtypeStruct((tracer_count, levels, rows, sector), f32),
-            scratch_shapes=[
-                pltpu.VMEM((rows * levels, length), jnp.bfloat16),
-                pltpu.VMEM((rows * levels, length), jnp.bfloat16),
-                pltpu.VMEM((rows * levels, length), f32),
-            ],
-            input_output_aliases={8: 0} if has_alias else {},
-            compiler_params=params(),
-            cost_estimate=cost(450_000_000, 3_000_000),
-            name="filter",
-        )(polar_mask, physics, other, *(jnp.asarray(table) for table in tables), scale, *([out] if has_alias else []))
-        if not last:
-            energy, out = lax.optimization_barrier((energy, out))
-
-    owner_energy = jnp.sum(owner_parts).reshape(1, 1) / (block_count * BLOCK)
+    tables = [jnp.asarray(table) for table in (others_high, others_low, first_high, first_low)]
+    distance = 1
+    for chunk in range(max(len(groups), lat_count.bit_length() - 1)):
+        if distance < lat_count:
+            received = lax.ppermute(energy, "lat", [(i, i ^ distance) for i in range(lat_count)])
+            distance *= 2
+        else:
+            received = None
+        if chunk < len(groups):
+            begin, end = groups[chunk]
+            has_alias = int(out is not None)
+            out = pl.pallas_call(
+                functools.partial(filter_kernel, rows, levels, sector, radix, has_alias),
+                grid=(end - begin,),
+                in_specs=[pl.BlockSpec(memory_space=pltpu.SMEM)]
+                + [whole] * (3 + len(tables))
+                + [pl.BlockSpec(memory_space=pl.ANY)] * has_alias,
+                out_specs=pl.BlockSpec((1, levels, rows, sector), lambda i, begin=begin: (begin + i, 0, 0, 0)),
+                out_shape=jax.ShapeDtypeStruct((tracer_count, levels, rows, sector), f32),
+                scratch_shapes=[
+                    pltpu.VMEM((rows * levels, length), jnp.bfloat16),
+                    pltpu.VMEM((rows * levels, length), jnp.bfloat16),
+                    pltpu.VMEM((rows * levels, length), f32),
+                ],
+                input_output_aliases={8: 0} if has_alias else {},
+                compiler_params=params(),
+                cost_estimate=cost(450_000_000, 3_000_000),
+                name="filter",
+            )(polar_mask, physics[chunk], other[chunk], *tables, scale, *([out] if has_alias else []))
+        if received is not None:
+            received, out = lax.optimization_barrier((received, out))
+            energy = energy + received
+        if chunk + 1 < len(groups):
+            energy, physics[chunk + 1] = lax.optimization_barrier((energy, physics[chunk + 1]))
+
+    owner_energy = jnp.sum(lax.dynamic_slice_in_dim(energy, lat, 1, 0)).reshape(1, 1) / (block_count * BLOCK)
     return out, owner_energy
 
 

time: 68 us -> 61.6 us (0.906)
  blocking collectives: 12.3 us -> 0 us
  waiting for transfers between devices: 13 us -> 18.3 us
  local copies, waits for them, and re-layouts: 10.2 us -> 5.65 us
  Pallas kernels: 14.9 us -> 17.3 us
  starting transfers between devices: 12.8 us -> 14.6 us
  other arithmetic: 1.33 us -> 2.78 us
    all_to_all x1 -> x0, blocking collectives: 12.3 us -> none  [on_device(): owner_parts = lax.all_to_all(energy, 'lat', 0, 0, tiled=True)]
    ppermute x6 -> x8, waiting for transfers between devices: 13 us -> 18.3 us  [the longest x1 18.3 us: on_device(): from_south = lax.ppermute(up, 'lat', upward)]
    unnamed x60 -> x38, local copies, waits for them, and re-layouts: 7.44 us -> 3.53 us
    ppermute x6 -> x8, starting transfers between devices: 12.7 us -> 14.6 us  [the longest x1 6.45 us: on_device(): from_south = lax.ppermute(up, 'lat', upward)]
    pallas_call x2 -> x3, Pallas kernels: 7.84 us -> 9.65 us  [on_device(): pl.pallas_call(functools.partial(filter_kernel, rows, levels, sector, rad...]
    concatenate x1, other arithmetic: 0.14 us -> 0.87 us  [on_device(): jnp.concatenate([ends, lon_end[None]], axis=0)]
    broadcast_in_dim x1, local copies, waits for them, and re-layouts: 0.01 us -> 0.74 us  [on_device(): decay = decay_rate[:, :, None]]
    mul x1, other arithmetic: 0.08 us -> 0.79 us  [on_device(): scale = damping * jnp.asarray(weights, f32)[None]]
  transfers between devices with their start and end apart: 7 -> 9, of which waited for: 3 -> 1; matrix products, arithmetic and copies ran while one was open for 6% -> 7% of each run, Pallas kernels for 12% -> 20%
where the time goes in v3:
time: 61.6 us; the launch traced here: 61.2 us
  waiting for transfers between devices  18.3 us (30%)
  Pallas kernels  17.3 us (28%)
  starting transfers between devices  14.6 us (24%)
  local copies, waits for them, and re-layouts  5.65 us (9%)
  other arithmetic  2.78 us (5%)
  between operations  2.7 us (4%)
    ppermute x1, waiting for transfers between devices, on_device(): from_south = lax.ppermute(up, 'lat', upward)  18.3 us
    pallas_call x3, Pallas kernels, on_device(): pl.pallas_call(functools.partial(filter_kernel, rows, levels, sector, rad...  9.65 us
    ppermute x1, starting transfers between devices, on_device(): from_south = lax.ppermute(up, 'lat', upward)  6.45 us
    ppermute x3, starting transfers between devices, on_device(): lax.ppermute(energy, 'lat', [(i, i ^ distance) for i in range(lat_count)])  6.16 us
    unnamed x38, local copies, waits for them, and re-layouts  3.53 us
    pallas_call x1, Pallas kernels, on_device(): pl.pallas_call(functools.partial(physics_kernel, groups, rows, levels, se...  2.86 us
    pallas_call x1, Pallas kernels, on_device(): pl.pallas_call(functools.partial(base_kernel, rows, width), grid=(tracer_...  2.68 us
    pallas_call x1, Pallas kernels, on_device(): pl.pallas_call(functools.partial(pack_kernel, tracer_count, rows, levels)...  2.06 us
  transfers between devices with their start and end apart: 9, of which 1 were waited for; matrix products, arithmetic and copies ran while one was open for 7% of the time, Pallas kernels for 20%

profile of v3, /device:TPU:0, one launch (start us, length us, event | category | flops | bytes accessed | tf_op | source)
XLA Modules:
  0.0 61.2 jit_solution(14759137168476348576)
XLA Ops:
  0.6 0.0 copy-start.2
  0.6 1.3 %copy-done.2 = f32[4,32,4,576]{3,2,1,0:T(4,128)S(1)} copy-done((f32[4,32,4,576]{3,2,1,0:T(4,128)S(1)}, f32[4,32,4,576]{3,2,1,0:T(4,128)}, u32[]{:S(2)}) %copy-start.2) | copy-done | bytes 1179672
  1.9 1.0 %copy-done.4 = f32[32,4,576]{2,1,0:T(4,128)S(1)} copy-done((f32[32,4,576]{2,1,0:T(4,128)S(1)}, f32[32,4,576]{2,1,0:T(4,128)}, u32[]{:S(2)}) %copy-start.4) | copy-done | bytes 294936
  2.9 2.1 %pack.1 = (f32[128,1152]{1,0:T(8,128)}, f32[144,1152]{1,0:T(8,128)}) custom-call(f32[4,32,4,576]{3,2,1,0:T(4,128)S(1)} %copy-done.2, f32[32,4,576]{2,1,0:T(4,128)S(1)} %copy-done.4), custom_call_target="tpu_custom_call" | custom-call | bytes 600000 | tf_op jit(solution)/shard_map/pack/pallas_call | solution.py:245
  5.0 1.3 %collective-permute-start.2 = (f32[144,1152]{1,0:T(8,128)}, f32[144,1152]{1,0:T(8,128)S(1)}, u32[]{:S(2)}, u32[]{:S(2)}) collective-permute-start(f32[144,1152]{1,0:T(8,128)} %get-tuple-element.22), channel_id=1, source_target_pairs={{2,0},{4,2},{6,4},{8,6},{10,8},{12,10},{14,12},{3,1},{5,3},{7,5},{... | collective-permute-start | bytes 1990664 | tf_op jit(solution)/shard_map/ppermute | solution.py:260
  6.3 0.0 copy-start.14
  6.3 6.5 %collective-permute-start.1 = (f32[128,1152]{1,0:T(8,128)}, f32[128,1152]{1,0:T(8,128)}, u32[]{:S(2)}, u32[]{:S(2)}) collective-permute-start(f32[128,1152]{1,0:T(8,128)} %get-tuple-element.21), channel_id=1, source_target_pairs={{0,2},{2,4},{4,6},{6,8},{8,10},{10,12},{12,14},{1,3},{3,5},{5,7},{... | collective-permute-start | bytes 1769480 | tf_op jit(solution)/shard_map/ppermute | solution.py:259
  12.8 0.0 copy-done.3
  12.8 0.1 copy.56
  12.9 0.0 copy-start.17
  12.9 0.0 copy-start.5
  12.9 0.1 fusion.2
  13.1 0.0 copy-done.14
  13.1 0.0 copy-start.16
  13.1 0.0 copy-start.15
  13.1 0.0 copy-start.18
  13.1 0.4 copy-done.17
  13.6 0.9 %pad_maximum_fusion.1 = f32[5,4,32,4]{3,2,1,0:T(8,128)} fusion(f32[1,4,32,4]{3,2,1,0:T(8,128)S(1)} %fusion.1, f32[4,4,32,2]{3,2,1,0:T(8,128)S(1)} %get-tuple-element.41, f32[4,4,32,2]{3,2,1,0:T(8,128)S(1)} %get-tuple-element.40), kind=kLoop, calls=%fused_computation.2 | loop fusion | flops 5120 | bytes 20480 | tf_op jit(solution)/shard_map/concatenate | solution.py:268
  14.4 0.0 collective-permute-start
  14.5 0.0 copy-done.5
  14.5 0.1 fusion
  14.6 0.1 pad.25.clone
  14.6 0.1 pad.22.clone
  14.8 0.0 copy-done.16
  14.8 0.7 %copy.50.refs_8_ = f32[4,32,1]{2,1,0:T(8,128)} copy(f32[4,32,1]{1,0,2:T(4,128)S(1)} %bitcast.19) | data formatting | bytes 1024 | tf_op jit(solution)/shard_map/broadcast_in_dim | solution.py:292
  15.5 0.0 copy-done.15
  15.5 0.6 %pad.19.refs_6_ = f32[4,4,640]{2,1,0:T(4,128)} pad(f32[4,4,576]{2,1,0:T(4,128)S(1)} %copy-done.15, f32[]{:T(128)} %constant.23.clone.1), padding=0_0x0_0x0_64 | pad | bytes 77828 | tf_op jit(solution)/shard_map/jit(_pad)/pad | solution.py:291
  16.1 0.0 copy-done.18
  16.1 0.1 broadcast_in_dim.40
  16.2 0.1 reshape_reshape.3
  16.3 0.0 collective-permute-done
  16.3 0.1 maximum_maximum_fusion.east_courant_ref
  16.4 0.1 fusion.3
  16.5 0.3 pad_maximum_fusion.padded_ref.refs_2_
  16.8 0.0 copy-start.12
  16.8 2.7 %base.1.refs_1_ = f32[4,4,32,640]{3,2,1,0:T(8,128)S(1)} custom-call(f32[4,4,32,640]{3,2,1,0:T(8,128)S(1)} %pad_maximum_fusion.padded_ref.refs_2_, f32[4,32,640]{2,1,0:T(8,128)S(1)} %maximum_maximum_fusion.east_courant_ref, f32[4,32,640]{2,1,0:T(8,128)S(1)} %pad.18.lat_courant_ref.refs_5_), custom_call_target="tpu_custom_call" | custom-call | bytes 3000000 | tf_op jit(solution)/shard_map/base/pallas_call | solution.py:276
  19.5 0.0 copy-start
  19.5 0.0 copy-start.1
  19.6 0.0 copy-start.6
  19.6 0.0 copy-start.7
  19.6 0.0 copy-start.13
  19.6 18.3 %collective-permute-done.1.refs_3_ = f32[128,1152]{1,0:T(8,128)} collective-permute-done((f32[128,1152]{1,0:T(8,128)}, f32[128,1152]{1,0:T(8,128)}, u32[]{:S(2)}, u32[]{:S(2)}) %collective-permute-start.1) | collective-permute-done | bytes 589856 | tf_op jit(solution)/shard_map/ppermute | solution.py:259
  37.8 0.0 collective-permute-done.2.refs_4_
  37.8 0.0 copy-done.10
  37.9 2.9 %physics.1 = (f32[1,4,32,640]{3,2,1,0:T(8,128)S(1)}, f32[1,4,32,640]{3,2,1,0:T(8,128)S(1)}, f32[2,4,32,640]{3,2,1,0:T(8,128)}, f32[8,128]{1,0:T(8,128)S(1)}) custom-call(s32[4,640]{1,0:T(4,128)S(1)} %pad.16.refs_0_, f32[4,4,32,640]{3,2,1,0:T(8,128)S(1)} %base.1.refs_1_, f32[4,4,32,640]{3,2,1,0:T(8,128)S(1)} %pad_maximum_fusion.padded_ref.refs_2_, ...), custom_call_target="tpu_custom_call" | custom-call | flops 50000000 | bytes 4000000 | tf_op jit(solution)/shard_map/physics/pallas_call | solution.py:309
  40.7 0.7 %copy-done.8 = f32[1,4,32,640]{3,2,1,0:T(8,128)} copy-done((f32[1,4,32,640]{3,2,1,0:T(8,128)}, f32[1,4,32,640]{3,2,1,0:T(8,128)S(1)}, u32[]{:S(2)}) %copy-start.8) | copy-done | bytes 327704
  41.5 0.0 collective-permute-start.8
  41.5 0.6 collective-permute-start.4
  42.1 0.1 collective-permute-start.6
  42.2 0.8 %select_multiply_fusion.refs_7_ = f32[4,1152]{1,0:T(4,128)S(1)} fusion(f32[1152]{0:T(1024)} %constant.54.clone, f32[1152]{0:T(1024)} %constant.52.clone, f32[4]{0:T(128)S(1)} %cosine_multiply_fusion, pred[1152]{0:T(1024)(128)(4,1)} %constant.53.clone), kind=kLoop, calls=%fused_computation.10 | loop fusion | flops 23040 | bytes 28816 | tf_op jit(solution)/shard_map/mul | solution.py:305
  43.0 2.6 %collective-permute-start.3 = (f32[8,128]{1,0:T(8,128)S(1)}, f32[8,128]{1,0:T(8,128)S(1)}, u32[]{:S(2)}, u32[]{:S(2)}) collective-permute-start(f32[8,128]{1,0:T(8,128)S(1)} %get-tuple-element.26), channel_id=1, source_target_pairs={{0,2},{2,0},{4,6},{6,4},{8,10},{10,8},{12,14},{14,12},{1,3},{3,1},... | collective-permute-start | bytes 12296 | tf_op jit(solution)/shard_map/ppermute | solution.py:325
  45.5 0.0 collective-permute-done.4.refs_2_
  45.5 0.0 copy-done
  45.6 2.6 %filter.3.refs_8_ = f32[4,32,4,576]{3,2,1,0:T(4,128)} custom-call(s32[4]{0:T(128)S(1)} %copy-done.13, f32[1,4,32,640]{3,2,1,0:T(8,128)S(1)} %get-tuple-element.27.refs_1_, f32[1,4,32,640]{3,2,1,0:T(8,128)S(1)} %collective-permute-done.4.refs_2_, bf16[2048,256]{1,0:T(8,128)(2,1)S(1)} %copy-done, bf16[2048,256]{1,0:T(8,128)(2,1)S(1)} %copy-done.1, ...), custom_call_target="tpu_custom_call" | custom-call | flops 450000000 | bytes 3000000 | tf_op jit(solution)/shard_map/filter/pallas_call | solution.py:332
  48.1 0.0 collective-permute-done.3
  48.1 1.6 %collective-permute-start.5 = (f32[8,128]{1,0:T(8,128)S(1)}, f32[8,128]{1,0:T(8,128)S(1)}, u32[]{:S(2)}, u32[]{:S(2)}) collective-permute-start(f32[8,128]{1,0:T(8,128)S(1)} %add.46), channel_id=1, source_target_pairs={{0,4},{2,6},{4,0},{6,2},{8,12},{10,14},{12,8},{14,10},{1,5},{3,7},... | collective-permute-start | bytes 12296 | tf_op jit(solution)/shard_map/ppermute | solution.py:325
  49.7 0.0 collective-permute-done.6.refs_2_
  49.7 2.6 %filter.4.refs_8_ = f32[4,32,4,576]{3,2,1,0:T(4,128)} custom-call(s32[4]{0:T(128)S(1)} %copy-done.13, f32[1,4,32,640]{3,2,1,0:T(8,128)S(1)} %copy-done.9, f32[1,4,32,640]{3,2,1,0:T(8,128)S(1)} %collective-permute-done.6.refs_2_, bf16[2048,256]{1,0:T(8,128)(2,1)S(1)} %copy-done, bf16[2048,256]{1,0:T(8,128)(2,1)S(1)} %copy-done.1, ...), custom_call_target="tpu_custom_call", output_to_operand_aliasing={{}: (8, {})} | custom-call | flops 450000000 | bytes 3000000 | tf_op jit(solution)/shard_map/filter/pallas_call | solution.py:332
  52.3 0.0 collective-permute-done.5
  52.3 2.0 %collective-permute-start.7 = (f32[8,128]{1,0:T(8,128)S(1)}, f32[8,128]{1,0:T(8,128)S(1)}, u32[]{:S(2)}, u32[]{:S(2)}) collective-permute-start(f32[8,128]{1,0:T(8,128)S(1)} %add.47), channel_id=1, source_target_pairs={{0,8},{2,10},{4,12},{6,14},{8,0},{10,2},{12,4},{14,6},{1,9},{3,11}... | collective-permute-start | bytes 12296 | tf_op jit(solution)/shard_map/ppermute | solution.py:325
  54.3 0.0 collective-permute-done.8.refs_2_
  54.4 4.5 %filter.5 = f32[4,32,4,576]{3,2,1,0:T(4,128)} custom-call(s32[4]{0:T(128)S(1)} %copy-done.13, f32[2,4,32,640]{3,2,1,0:T(8,128)} %get-tuple-element.36.refs_1_, f32[2,4,32,640]{3,2,1,0:T(8,128)S(1)} %collective-permute-done.8.refs_2_, bf16[2048,256]{1,0:T(8,128)(2,1)S(1)} %copy-done, bf16[2048,256]{1,0:T(8,128)(2,1)S(1)} %copy-done.1, ...), custom_call_target="tpu_custom_call", output_to_operand_aliasing={{}: (8, {})} | custom-call | flops 450000000 | bytes 3000000 | tf_op jit(solution)/shard_map/filter/pallas_call | solution.py:332
  58.8 0.0 collective-permute-done.7
  58.8 0.6 dynamic-slice_reduce_fusion
  (25 shorter events, 0.2 us)
Async XLA Ops:
  0.6 1.3 %copy-start.2 = (f32[4,32,4,576]{3,2,1,0:T(4,128)S(1)}, f32[4,32,4,576]{3,2,1,0:T(4,128)}, u32[]{:S(2)}) copy-start(f32[4,32,4,576]{3,2,1,0:T(4,128)} %tracer_hbm.1) | copy-start | bytes 3538948
  1.9 1.0 %copy-start.4 = (f32[32,4,576]{2,1,0:T(4,128)S(1)}, f32[32,4,576]{2,1,0:T(4,128)}, u32[]{:S(2)}) copy-start(f32[32,4,576]{2,1,0:T(4,128)} %courant_hbm.1) | copy-start | bytes 884740
  2.9 9.8 %copy-start.3 = (f32[4,32,4,576]{3,2,1,0:T(4,128)S(1)}, f32[4,32,4,576]{3,2,1,0:T(4,128)}, u32[]{:S(2)}) copy-start(f32[4,32,4,576]{3,2,1,0:T(4,128)} %tracer_hbm.1) | copy-start | bytes 3538948
  5.0 32.9 %collective-permute-start.2 = (f32[144,1152]{1,0:T(8,128)}, f32[144,1152]{1,0:T(8,128)S(1)}, u32[]{:S(2)}, u32[]{:S(2)}) collective-permute-start(f32[144,1152]{1,0:T(8,128)} %get-tuple-element.22), channel_id=1, source_target_pairs={{2,0},{4,2},{6,4},{8,6},{10,8},{12,10},{14,12},{3,1},{5,3},{7,5},{... | collective-permute-start | bytes 1990664 | tf_op jit(solution)/shard_map/ppermute | solution.py:260
  6.3 6.8 %copy-start.14 = (f32[32,4,576]{2,1,0:T(4,128)S(1)}, f32[32,4,576]{2,1,0:T(4,128)}, u32[]{:S(2)}) copy-start(f32[32,4,576]{2,1,0:T(4,128)} %param.17) | copy-start | bytes 884740
  6.3 31.5 %collective-permute-start.1 = (f32[128,1152]{1,0:T(8,128)}, f32[128,1152]{1,0:T(8,128)}, u32[]{:S(2)}, u32[]{:S(2)}) collective-permute-start(f32[128,1152]{1,0:T(8,128)} %get-tuple-element.21), channel_id=1, source_target_pairs={{0,2},{2,4},{4,6},{6,8},{8,10},{10,12},{12,14},{1,3},{3,5},{5,7},{... | collective-permute-start | bytes 1769480 | tf_op jit(solution)/shard_map/ppermute | solution.py:259
  12.9 0.7 %copy-start.17 = (pred[4]{0:T(512)(128)(4,1)S(1)}, pred[4]{0:T(512)(128)(4,1)}, u32[]{:S(2)}) copy-start(pred[4]{0:T(512)(128)(4,1)} %constant.22.clone.1) | copy-start | bytes 16
  12.9 1.5 %copy-start.5 = (f32[32,4,576]{2,1,0:T(4,128)S(1)}, f32[32,4,576]{2,1,0:T(4,128)}, u32[]{:S(2)}) copy-start(f32[32,4,576]{2,1,0:T(4,128)} %courant_hbm.1) | copy-start | bytes 884740
  13.1 1.7 %copy-start.16 = (f32[4,32]{1,0:T(4,128)S(1)}, f32[4,32]{1,0:T(4,128)}, u32[]{:S(2)}) copy-start(f32[4,32]{1,0:T(4,128)} %param.20) | copy-start | bytes 1540
  13.1 2.4 %copy-start.15 = (f32[4,4,576]{2,1,0:T(4,128)S(1)}, f32[4,4,576]{2,1,0:T(4,128)}, u32[]{:S(2)}) copy-start(f32[4,4,576]{2,1,0:T(4,128)} %param.18) | copy-start | bytes 110596
  13.1 3.0 %copy-start.18 = (s32[1,1,18,1]{2,3,1,0:T(1,128)S(1)}, s32[1,1,18,1]{2,3,1,0:T(1,128)}, u32[]{:S(2)}) copy-start(s32[1,1,18,1]{2,3,1,0:T(1,128)} %param.21) | copy-start | bytes 220
  14.4 1.8 %collective-permute-start = (f32[5,4,32,4]{3,2,1,0:T(8,128)}, f32[5,4,32,4]{3,2,1,0:T(8,128)S(1)}, u32[]{:S(2)}, u32[]{:S(2)}) collective-permute-start(f32[5,4,32,4]{3,2,1,0:T(8,128)} %pad_maximum_fusion.1), channel_id=1, source_target_pairs={{0,1},{1,0},{2,3},{3,2},{4,5},{5,4},{6,7},{7,6},{8,9},{9,8},{10,11... | collective-permute-start | bytes 30728 | tf_op jit(solution)/shard_map/ppermute | solution.py:268
  16.8 21.0 %copy-start.10 = (f32[4,32,1]{2,1,0:T(8,128)S(1)}, f32[4,32,1]{2,1,0:T(8,128)}, u32[]{:S(2)}) copy-start(f32[4,32,1]{2,1,0:T(8,128)} %copy.50.refs_8_) | copy-start | bytes 1540
  16.8 21.0 %copy-start.11 = (f32[4,4,640]{2,1,0:T(4,128)S(1)}, f32[4,4,640]{2,1,0:T(4,128)}, u32[]{:S(2)}) copy-start(f32[4,4,640]{2,1,0:T(4,128)} %pad.19.refs_6_) | copy-start | bytes 122884
  16.8 21.0 %copy-start.12 = (f32[32,32]{1,0:T(8,128)S(1)}, f32[32,32]{1,0:T(8,128)}, u32[]{:S(2)}) copy-start(f32[32,32]{1,0:T(8,128)} %refs_7_.1) | copy-start | bytes 12292
  19.5 26.0 %copy-start = (bf16[2048,256]{1,0:T(8,128)(2,1)S(1)}, bf16[2048,256]{1,0:T(8,128)(2,1)}, u32[]{:S(2)}) copy-start(bf16[2048,256]{1,0:T(8,128)(2,1)} %constant.55.clone.refs_3_) | copy-start | bytes 3145732
  19.5 26.0 %copy-start.1 = (bf16[2048,256]{1,0:T(8,128)(2,1)S(1)}, bf16[2048,256]{1,0:T(8,128)(2,1)}, u32[]{:S(2)}) copy-start(bf16[2048,256]{1,0:T(8,128)(2,1)} %constant.56.clone.refs_4_) | copy-start | bytes 3145732
  19.6 26.0 %copy-start.6 = (bf16[256,128]{1,0:T(8,128)(2,1)S(1)}, bf16[256,128]{1,0:T(8,128)(2,1)}, u32[]{:S(2)}) copy-start(bf16[256,128]{1,0:T(8,128)(2,1)} %constant.57.clone.refs_5_) | copy-start | bytes 196612
  19.6 26.0 %copy-start.7 = (bf16[256,128]{1,0:T(8,128)(2,1)S(1)}, bf16[256,128]{1,0:T(8,128)(2,1)}, u32[]{:S(2)}) copy-start(bf16[256,128]{1,0:T(8,128)(2,1)} %constant.58.clone.refs_6_) | copy-start | bytes 196612
  19.6 26.0 %copy-start.13 = (s32[4]{0:T(128)S(1)}, s32[4]{0:T(128)}, u32[]{:S(2)}) copy-start(s32[4]{0:T(128)} %refs_0_.5) | copy-start | bytes 52
  40.7 0.7 %copy-start.8 = (f32[1,4,32,640]{3,2,1,0:T(8,128)}, f32[1,4,32,640]{3,2,1,0:T(8,128)S(1)}, u32[]{:S(2)}) copy-start(f32[1,4,32,640]{3,2,1,0:T(8,128)S(1)} %get-tuple-element.31.refs_1_) | copy-start | bytes 983044
  41.5 12.9 %collective-permute-start.8 = (f32[2,4,32,640]{3,2,1,0:T(8,128)}, f32[2,4,32,640]{3,2,1,0:T(8,128)S(1)}, u32[]{:S(2)}, u32[]{:S(2)}) collective-permute-start(f32[2,4,32,640]{3,2,1,0:T(8,128)} %get-tuple-element.36.refs_1_), channel_id=1, source_target_pairs={{0,1},{1,0},{2,3},{3,2},{4,5},{5,4},{6,7},{7,6},{8,9},{9,8},{10,11... | collective-permute-start | bytes 1966088 | tf_op jit(solution)/shard_map/ppermute | solution.py:318
  41.5 4.0 %collective-permute-start.4 = (f32[1,4,32,640]{3,2,1,0:T(8,128)S(1)}, f32[1,4,32,640]{3,2,1,0:T(8,128)S(1)}, u32[]{:S(2)}, u32[]{:S(2)}) collective-permute-start(f32[1,4,32,640]{3,2,1,0:T(8,128)S(1)} %get-tuple-element.27.refs_1_), channel_id=1, source_target_pairs={{0,1},{1,0},{2,3},{3,2},{4,5},{5,4},{6,7},{7,6},{8,9},{9,8},{10,11... | collective-permute-start | bytes 983048 | tf_op jit(solution)/shard_map/ppermute | solution.py:318
  42.1 7.6 %collective-permute-start.6 = (f32[1,4,32,640]{3,2,1,0:T(8,128)}, f32[1,4,32,640]{3,2,1,0:T(8,128)S(1)}, u32[]{:S(2)}, u32[]{:S(2)}) collective-permute-start(f32[1,4,32,640]{3,2,1,0:T(8,128)} %copy-done.8), channel_id=1, source_target_pairs={{0,1},{1,0},{2,3},{3,2},{4,5},{5,4},{6,7},{7,6},{8,9},{9,8},{10,11... | collective-permute-start | bytes 983048 | tf_op jit(solution)/shard_map/ppermute | solution.py:318
  43.0 6.8 %copy-start.9 = (f32[1,4,32,640]{3,2,1,0:T(8,128)S(1)}, f32[1,4,32,640]{3,2,1,0:T(8,128)}, u32[]{:S(2)}) copy-start(f32[1,4,32,640]{3,2,1,0:T(8,128)} %copy-done.8) | copy-start | bytes 983044
  43.0 5.2 %collective-permute-start.3 = (f32[8,128]{1,0:T(8,128)S(1)}, f32[8,128]{1,0:T(8,128)S(1)}, u32[]{:S(2)}, u32[]{:S(2)}) collective-permute-start(f32[8,128]{1,0:T(8,128)S(1)} %get-tuple-element.26), channel_id=1, source_target_pairs={{0,2},{2,0},{4,6},{6,4},{8,10},{10,8},{12,14},{14,12},{1,3},{3,1},... | collective-permute-start | bytes 12296 | tf_op jit(solution)/shard_map/ppermute | solution.py:325
  48.1 4.2 %collective-permute-start.5 = (f32[8,128]{1,0:T(8,128)S(1)}, f32[8,128]{1,0:T(8,128)S(1)}, u32[]{:S(2)}, u32[]{:S(2)}) collective-permute-start(f32[8,128]{1,0:T(8,128)S(1)} %add.46), channel_id=1, source_target_pairs={{0,4},{2,6},{4,0},{6,2},{8,12},{10,14},{12,8},{14,10},{1,5},{3,7},... | collective-permute-start | bytes 12296 | tf_op jit(solution)/shard_map/ppermute | solution.py:325
  52.3 6.5 %collective-permute-start.7 = (f32[8,128]{1,0:T(8,128)S(1)}, f32[8,128]{1,0:T(8,128)S(1)}, u32[]{:S(2)}, u32[]{:S(2)}) collective-permute-start(f32[8,128]{1,0:T(8,128)S(1)} %add.47), channel_id=1, source_target_pairs={{0,8},{2,10},{4,12},{6,14},{8,0},{10,2},{12,4},{14,6},{1,9},{3,11}... | collective-permute-start | bytes 12296 | tf_op jit(solution)/shard_map/ppermute | solution.py:325
